TPU v7x, 32 devices: a whole 2x2x4 slice. The times are simulated.
32 devices in a mesh: dp: 8 (over z, x), tensor: 4 (over y, core).
Axes of the slice: x: 2, y: 2, z: 4, core: 2. Of those that a mesh axis runs over, the one named last changes fastest.
Arguments:
- block_input: bfloat16 [8192, 768], P(('dp', 'tensor')), may hold values from -6 to 6
- out_cotangent: bfloat16 [8192, 768], P(('dp', 'tensor')), may hold values from -6 to 6
- seq_lengths: int32 [8, 4], replicated, may hold values from 1 to 682, 1024 in all within a row
- pack_order: int32 [8], replicated, may hold values from 0 to 7, each once
- ln1_gain: float32 [768], replicated, may hold values from 0.5 to 1.5
- ln1_bias: float32 [768], replicated, may hold values from -1.5 to 1.5
- qkv_weight: float32 [768, 3, 768], P('dp', None, 'tensor'), may hold values from -0.21875 to 0.21875
- qv_bias: float32 [2, 768], P(None, 'tensor'), may hold values from -1.5 to 1.5
- attn_out_weight: float32 [768, 768], P('tensor', 'dp'), may hold values from -1.75 to 1.75
- attn_out_bias: float32 [768], replicated, may hold values from -1.5 to 1.5
- ln2_gain: float32 [768], replicated, may hold values from 0.5 to 1.5
- ln2_bias: float32 [768], replicated, may hold values from -1.5 to 1.5
- fc_weight: float32 [768, 3072], P('dp', 'tensor'), may hold values from -0.21875 to 0.21875
- fc_bias: float32 [3072], P('tensor'), may hold values from -1.5 to 1.5
- proj_weight: float32 [3072, 768], P('tensor', 'dp'), may hold values from -0.109375 to 0.109375
- proj_bias: float32 [768], replicated, may hold values from -1.5 to 1.5
Outputs:
- block_output: bfloat16 [8192, 768], P(('dp', 'tensor'))
- input_grad: bfloat16 [8192, 768], P(('dp', 'tensor'))
- ln1_gain_grad: float32 [768], replicated
- ln1_bias_grad: float32 [768], replicated
- qkv_weight_grad: float32 [768, 3, 768], P('dp', None, 'tensor')
- qv_bias_grad: float32 [2, 768], P(None, 'tensor')
- attn_out_weight_grad: float32 [768, 768], P('tensor', 'dp')
- attn_out_bias_grad: float32 [768], replicated
- ln2_gain_grad: float32 [768], replicated
- ln2_bias_grad: float32 [768], replicated
- fc_weight_grad: float32 [768, 3072], P('dp', 'tensor')
- fc_bias_grad: float32 [3072], P('tensor')
- proj_weight_grad: float32 [3072, 768], P('tensor', 'dp')
- proj_bias_grad: float32 [768], replicated
Inputs may be any that keep to these rules, and one draw needn't show every extreme that they name: `seq_lengths`: each row gives the lengths of the 4 sequences of one pack in order, sums to 1024, and its largest entry is 682. `pack_order`: a permutation of the 8 packs.
All inputs are finite; a program needn't handle non-finite values.
Results may differ from a plain program's by a relative error of at most 0.017.
Values may be sent and summed in bfloat16 or wider, within the bound.
A program may use at most 128 MiB of HBM per device.

v0:
```python
import jax
import jax.numpy as jnp
from jax import lax
from jax.sharding import PartitionSpec as P

HEAD_DIM = 64


EPSILON = 1e-05
MASKED = -1e30


def gelu_curve(values):
    return (
        0.5
        * values
        * (1.0 + jnp.tanh(0.7978845608028654 * (values + 0.044715 * values * values * values)))
    )


def contract(left_side, right_side, left_dim, right_dim):
    return lax.dot_general(
        left_side,
        right_side,
        (((left_dim,), (right_dim,)), ((), ())),
        preferred_element_type=jnp.float32,
    )


def normalize(rows_in, norm_gain, norm_bias):
    row_mean = jnp.mean(rows_in, axis=1, keepdims=True)
    row_var = jnp.mean(rows_in * rows_in, axis=1, keepdims=True) - row_mean * row_mean
    row_scale = lax.rsqrt(row_var + EPSILON)
    centered = (rows_in - row_mean) * row_scale
    return (centered, row_scale, (centered * norm_gain + norm_bias).astype(jnp.bfloat16))


def norm_back(grad_in, centered, row_scale, norm_gain):
    gain_grad = jnp.sum(grad_in * centered, axis=0)
    bias_grad = jnp.sum(grad_in, axis=0)
    scaled = grad_in * norm_gain
    back = row_scale * (
        scaled
        - jnp.mean(scaled, axis=1, keepdims=True)
        - centered * jnp.mean(scaled * centered, axis=1, keepdims=True)
    )
    return (back, gain_grad, bias_grad)


def grad_rows(local_rows):
    return lax.all_gather(local_rows, "tensor", axis=0, tiled=True)


def input_total(partial_value):
    return lax.psum_scatter(
        partial_value.astype(jnp.bfloat16), "tensor", scatter_dimension=0, tiled=True
    ).astype(jnp.float32)


def block_scores(query_rows, keys_seen, segment, begin_row):
    block_len = query_rows.shape[0]
    key_count = keys_seen.shape[0]
    row_pos = begin_row + jnp.arange(block_len, dtype=jnp.int32)
    col_pos = jnp.arange(key_count, dtype=jnp.int32)
    row_segment = segment[begin_row : begin_row + block_len]
    allowed = (col_pos[None, :] <= row_pos[:, None]) & (
        segment[None, :key_count] == row_segment[:, None]
    )
    raw_scores = jnp.einsum(
        "qhd,khd->hqk", query_rows, keys_seen, preferred_element_type=jnp.float32
    ) * query_rows.shape[2] ** (-0.5)
    return jnp.where(allowed[None], raw_scores, MASKED)


def attend(queries, keys_all, values_all, segment, block_len):
    outputs = []
    log_totals = []
    for begin_row in range(0, queries.shape[0], block_len):
        final_row = begin_row + block_len
        query_rows = queries[begin_row:final_row]
        scores = block_scores(query_rows, keys_all[:final_row], segment, begin_row)
        row_peak = jnp.max(scores, axis=-1, keepdims=True)
        weights = jnp.exp(scores - row_peak)
        weight_total = jnp.sum(weights, axis=-1, keepdims=True)
        probs = (weights / weight_total).astype(jnp.bfloat16)
        outputs.append(
            jnp.einsum(
                "hqk,khd->qhd", probs, values_all[:final_row], preferred_element_type=jnp.float32
            )
        )
        log_totals.append(row_peak + jnp.log(weight_total))
    return (jnp.concatenate(outputs, axis=0), log_totals)


def attend_back(queries, keys_all, values_all, segment, block_len, log_totals, out_grad):
    factor = queries.shape[2] ** (-0.5)
    key_grad = jnp.zeros(keys_all.shape, jnp.float32)
    value_grad = jnp.zeros(values_all.shape, jnp.float32)
    query_grads = []
    for block_index, begin_row in enumerate(range(0, queries.shape[0], block_len)):
        final_row = begin_row + block_len
        query_rows = queries[begin_row:final_row]
        keys_seen = keys_all[:final_row]
        values_seen = values_all[:final_row]
        grad_block = out_grad[begin_row:final_row]
        probs = jnp.exp(
            block_scores(query_rows, keys_seen, segment, begin_row) - log_totals[block_index]
        )
        value_grad = value_grad.at[:final_row].add(
            jnp.einsum(
                "hqk,qhd->khd",
                probs.astype(jnp.bfloat16),
                grad_block,
                preferred_element_type=jnp.float32,
            )
        )
        prob_grad = jnp.einsum(
            "qhd,khd->hqk", grad_block, values_seen, preferred_element_type=jnp.float32
        )
        row_delta = jnp.sum(probs * prob_grad, axis=-1, keepdims=True)
        score_grad = (probs * (prob_grad - row_delta)).astype(jnp.bfloat16)
        query_grads.append(
            jnp.einsum("hqk,khd->qhd", score_grad, keys_seen, preferred_element_type=jnp.float32)
            * factor
        )
        key_grad = key_grad.at[:final_row].add(
            jnp.einsum("hqk,qhd->khd", score_grad, query_rows, preferred_element_type=jnp.float32)
            * factor
        )
    return (jnp.concatenate(query_grads, axis=0), key_grad, value_grad)


def local(
    block_input,
    out_cotangent,
    seq_lengths,
    pack_order,
    ln1_gain,
    ln1_bias,
    qkv_weight,
    qv_bias,
    attn_out_weight,
    attn_out_bias,
    ln2_gain,
    ln2_bias,
    fc_weight,
    fc_bias,
    proj_weight,
    proj_bias,
):
    local_rows, width = block_input.shape
    pack_count = pack_order.shape[0]
    piece_rows = local_rows // pack_count
    pack_rows = local_rows * lax.axis_size("tensor")
    head_cols = qv_bias.shape[1]
    heads_here = head_cols // HEAD_DIM
    block_len = min(512, pack_rows)
    slots = jnp.arange(pack_count, dtype=jnp.int32)
    inverse = jnp.sum(jnp.where(pack_order[None, :] == slots[:, None], slots[None, :], 0), axis=1)
    sent_input = jnp.take(
        block_input.reshape(pack_count, piece_rows, width), inverse, axis=0
    ).reshape(local_rows, width)
    sent_grad = jnp.take(
        out_cotangent.reshape(pack_count, piece_rows, width), inverse, axis=0
    ).reshape(local_rows, width)
    arrived = (
        lax.all_to_all(sent_input, "dp", split_axis=0, concat_axis=0, tiled=True),
        lax.all_to_all(sent_grad, "dp", split_axis=0, concat_axis=0, tiled=True),
    )
    input_here = arrived[0].astype(jnp.float32)
    grad_here = arrived[1].astype(jnp.float32)
    my_pack = lax.axis_index("dp")
    my_lengths = lax.dynamic_index_in_dim(seq_lengths, my_pack, 0, keepdims=False)
    seq_ends = jnp.cumsum(my_lengths)
    positions = jnp.arange(pack_rows, dtype=jnp.int32)
    segment = jnp.sum((positions[:, None] >= seq_ends[None, :]).astype(jnp.int32), axis=1)
    weights = (
        lax.all_gather(qkv_weight.astype(jnp.bfloat16), "dp", axis=0, tiled=True),
        lax.all_gather(attn_out_weight.astype(jnp.bfloat16), "dp", axis=1, tiled=True),
        lax.all_gather(fc_weight.astype(jnp.bfloat16), "dp", axis=0, tiled=True),
        lax.all_gather(proj_weight.astype(jnp.bfloat16), "dp", axis=1, tiled=True),
    )
    qkv_full = weights[0].reshape(width, 3 * head_cols)
    out_full = weights[1]
    fc_full = weights[2]
    proj_full = weights[3]
    centered_one, scale_one, ln_one = normalize(input_here, ln1_gain, ln1_bias)
    normed_one = lax.all_gather(ln_one, "tensor", axis=0, tiled=True)
    projected = jnp.dot(normed_one, qkv_full, preferred_element_type=jnp.float32)
    queries = (
        (projected[:, :head_cols] + qv_bias[0])
        .astype(jnp.bfloat16)
        .reshape(pack_rows, heads_here, HEAD_DIM)
    )
    keys_all = (
        projected[:, head_cols : 2 * head_cols]
        .astype(jnp.bfloat16)
        .reshape(pack_rows, heads_here, HEAD_DIM)
    )
    values_all = (
        (projected[:, 2 * head_cols :] + qv_bias[1])
        .astype(jnp.bfloat16)
        .reshape(pack_rows, heads_here, HEAD_DIM)
    )
    attended, log_totals = attend(queries, keys_all, values_all, segment, block_len)
    attended_low = attended.reshape(pack_rows, head_cols).astype(jnp.bfloat16)
    attn_partial = jnp.dot(attended_low, out_full, preferred_element_type=jnp.float32)
    attn_here = lax.psum_scatter(
        attn_partial.astype(jnp.bfloat16), "tensor", scatter_dimension=0, tiled=True
    ).astype(jnp.float32)
    resid_one = input_here + attn_here + attn_out_bias
    centered_two, scale_two, ln_two = normalize(resid_one, ln2_gain, ln2_bias)
    normed_two = lax.all_gather(ln_two, "tensor", axis=0, tiled=True)
    upper_pre = jnp.dot(normed_two, fc_full, preferred_element_type=jnp.float32) + fc_bias
    activated = gelu_curve(upper_pre).astype(jnp.bfloat16)
    mlp_here = lax.psum_scatter(
        jnp.dot(activated, proj_full, preferred_element_type=jnp.float32).astype(jnp.bfloat16),
        "tensor",
        scatter_dimension=0,
        tiled=True,
    ).astype(jnp.float32)
    block_output = (resid_one + mlp_here + proj_bias).astype(jnp.bfloat16)
    proj_bias_grad = jnp.sum(grad_here, axis=0)
    mlp_grad = grad_rows(grad_here.astype(jnp.bfloat16))
    proj_grad = contract(activated, mlp_grad, 0, 0)
    act_grad = contract(mlp_grad, proj_full, 1, 1)
    gelu_pull = jax.vjp(gelu_curve, upper_pre)[1]
    upper_grad = gelu_pull(act_grad)[0].astype(jnp.bfloat16)
    fc_bias_grad = jnp.sum(upper_grad.astype(jnp.float32), axis=0)
    fc_grad = contract(normed_two, upper_grad, 0, 0)
    normed_two_grad = input_total(contract(upper_grad, fc_full, 1, 1))
    back_two, ln2_gain_grad, ln2_bias_grad = norm_back(
        normed_two_grad, centered_two, scale_two, ln2_gain
    )
    resid_grad = grad_here + back_two
    attn_out_bias_grad = jnp.sum(resid_grad, axis=0)
    attn_grad_rows = grad_rows(resid_grad.astype(jnp.bfloat16))
    out_weight_grad = contract(attended_low, attn_grad_rows, 0, 0)
    attended_grad = (
        contract(attn_grad_rows, out_full, 1, 1)
        .astype(jnp.bfloat16)
        .reshape(pack_rows, heads_here, HEAD_DIM)
    )
    query_grad, key_grad, value_grad = attend_back(
        queries, keys_all, values_all, segment, block_len, log_totals, attended_grad
    )
    query_low = query_grad.reshape(pack_rows, head_cols).astype(jnp.bfloat16)
    key_low = key_grad.reshape(pack_rows, head_cols).astype(jnp.bfloat16)
    value_low = value_grad.reshape(pack_rows, head_cols).astype(jnp.bfloat16)
    qv_bias_grad = jnp.stack(
        [
            jnp.sum(query_low.astype(jnp.float32), axis=0),
            jnp.sum(value_low.astype(jnp.float32), axis=0),
        ]
    )
    joined_grad = jnp.concatenate([query_low, key_low, value_low], axis=1)
    qkv_grad = contract(normed_one, joined_grad, 0, 0).reshape(width, 3, head_cols)
    normed_one_grad = input_total(contract(joined_grad, qkv_full, 1, 1))
    back_one, ln1_gain_grad, ln1_bias_grad = norm_back(
        normed_one_grad, centered_one, scale_one, ln1_gain
    )
    input_grad = (resid_grad + back_one).astype(jnp.bfloat16)
    returned = (
        lax.all_to_all(block_output, "dp", split_axis=0, concat_axis=0, tiled=True),
        lax.all_to_all(input_grad, "dp", split_axis=0, concat_axis=0, tiled=True),
    )
    out_rows = jnp.take(
        returned[0].reshape(pack_count, piece_rows, width), pack_order, axis=0
    ).reshape(local_rows, width)
    grad_out_rows = jnp.take(
        returned[1].reshape(pack_count, piece_rows, width), pack_order, axis=0
    ).reshape(local_rows, width)
    all_sums = (
        lax.psum_scatter(qkv_grad, "dp", scatter_dimension=0, tiled=True),
        lax.psum_scatter(out_weight_grad, "dp", scatter_dimension=1, tiled=True),
        lax.psum_scatter(fc_grad, "dp", scatter_dimension=0, tiled=True),
        lax.psum_scatter(proj_grad, "dp", scatter_dimension=1, tiled=True),
    )
    qkv_sum, out_sum, fc_sum, proj_sum = (all_sums[0], all_sums[1], all_sums[2], all_sums[3])
    head_sums = lax.psum((qv_bias_grad, fc_bias_grad), "dp")
    shared_sums = lax.psum(
        (
            ln1_gain_grad,
            ln1_bias_grad,
            attn_out_bias_grad,
            ln2_gain_grad,
            ln2_bias_grad,
            proj_bias_grad,
        ),
        ("dp", "tensor"),
    )
    return (
        out_rows,
        grad_out_rows,
        shared_sums[0],
        shared_sums[1],
        qkv_sum,
        head_sums[0],
        out_sum,
        shared_sums[2],
        shared_sums[3],
        shared_sums[4],
        fc_sum,
        head_sums[1],
        proj_sum,
        shared_sums[5],
    )


def solution(mesh):
    return jax.shard_map(
        local,
        mesh=mesh,
        in_specs=(
            P(("dp", "tensor"), None),
            P(("dp", "tensor"), None),
            P(),
            P(),
            P(),
            P(),
            P("dp", None, "tensor"),
            P(None, "tensor"),
            P("tensor", "dp"),
            P(),
            P(),
            P(),
            P("dp", "tensor"),
            P("tensor"),
            P("tensor", "dp"),
            P(),
        ),
        out_specs=(
            P(("dp", "tensor"), None),
            P(("dp", "tensor"), None),
            P(),
            P(),
            P("dp", None, "tensor"),
            P(None, "tensor"),
            P("tensor", "dp"),
            P(),
            P(),
            P(),
            P("dp", "tensor"),
            P("tensor"),
            P("tensor", "dp"),
            P(),
        ),
        check_vma=False,
    )
```

profile of v0, /device:TPU:0, one launch (start us, length us, event | category | flops | bytes accessed | tf_op | source)
XLA Modules:
  0.0 679.9 jit_solution(4538594426250467787)
XLA Ops:
  8.1 0.9 select_reduce_fusion
  9.6 1.6 gather_fusion
  11.2 0.9 broadcast_select_fusion.2
  12.1 19.1 %all_to_all.33 = bf16[8,32,768]{2,1,0:T(8,128)(2,1)S(1)} all-to-all(bf16[8,32,768]{2,1,0:T(8,128)(2,1)S(1)} %get-tuple-element.121), channel_id=1, replica_groups=mesh['dp'=8,'tensor'=4] {'dp'}, dimensions={0} | all-to-all | bytes 786432 | tf_op jit(solution)/shard_map/all_to_all | solution.py:167
  31.6 1.0 fusion.66
  33.3 36.0 %all_gather.25 = bf16[768,3,192]{2,1,0:T(4,128)(2,1)S(1)} all-gather(bf16[96,3,192]{2,1,0:T(4,128)(2,1)S(1)} %copy.57), channel_id=1, replica_groups=mesh['dp'=8,'tensor'=4] {'dp'}, dimensions={0}, use_global_device_ids=true | all-gather | bytes 995328 | tf_op jit(solution)/shard_map/all_gather | solution.py:178
  69.3 0.9 copy.58
  70.3 33.0 %all_gather.26 = bf16[192,768]{0,1:T(8,128)(2,1)} all-gather(bf16[192,96]{0,1:T(8,128)(2,1)S(1)} %copy.60), channel_id=1, replica_groups=mesh['dp'=8,'tensor'=4] {'dp'}, dimensions={1}, use_global_device_ids=true | all-gather | bytes 331776 | tf_op jit(solution)/shard_map/all_gather | solution.py:179
  103.3 0.9 fusion.47
  104.3 1.3 fusion.14
  105.5 2.5 fusion.80
  109.1 0.8 fusion.82
  111.4 1.4 fusion.81
  112.9 1.5 fusion
  114.4 1.1 copy-done.2
  115.5 1.7 fusion.39
  118.0 1.8 convolution_convert_fusion.3
  119.9 1.6 convert_element_type.155
  121.6 25.3 %reduce-scatter.11.cloned.1.call-done = bf16[256,768]{1,0:T(8,128)(2,1)} async-done(((bf16[1024,768]{1,0:T(8,128)(2,1)}), bf16[256,768]{1,0:T(8,128)(2,1)}) %reduce-scatter.11.cloned.1.call-update) | async-done | bytes 393232 | tf_op jit(solution)/shard_map/reduce_scatter | solution.py:208
  146.9 1.3 fusion.69
  148.8 2.0 add_convert_fusion.1
  150.9 1.6 convert_element_type.157
  152.6 18.5 %all_to_all.34 = bf16[8,32,768]{2,1,0:T(8,128)(2,1)} all-to-all(bf16[8,32,768]{2,1,0:T(8,128)(2,1)} %get-tuple-element.120), channel_id=1, replica_groups=mesh['dp'=8,'tensor'=4] {'dp'}, dimensions={0} | all-to-all | bytes 786432 | tf_op jit(solution)/shard_map/all_to_all | solution.py:168
  171.4 14.1 %all-gather.9.cloned.1.call-done = bf16[1024,768]{1,0:T(8,128)(2,1)} async-done(((bf16[256,768]{1,0:T(8,128)(2,1)}), bf16[1024,768]{1,0:T(8,128)(2,1)}) %all-gather.9.cloned.1.call-update) | async-done | bytes 1572880 | tf_op jit(solution)/shard_map/all_gather | solution.py:213
  185.5 4.9 fusion.83
  190.4 39.0 %all-gather.13.cloned.1.call-done = bf16[768,768]{0,1:T(8,128)(2,1)} async-done(((bf16[768,96]{0,1:T(8,128)(2,1)}), bf16[768,768]{0,1:T(8,128)(2,1)}) %all-gather.13.cloned.1.call-update) | async-done | bytes 1179664 | tf_op jit(solution)/shard_map/all_gather | solution.py:181
  229.3 19.7 %all-gather.15.cloned.1.call-done = bf16[1024,768]{1,0:T(8,128)(2,1)} async-done(((bf16[256,768]{1,0:T(8,128)(2,1)}), bf16[1024,768]{1,0:T(8,128)(2,1)}) %all-gather.15.cloned.1.call-update) | async-done | bytes 1572880 | tf_op jit(solution)/shard_map/all_gather | solution.py:51
  249.0 6.9 %convert_reduce_fusion = (f32[768]{0:T(1024)}, bf16[1024,768]{1,0:T(8,128)(2,1)S(1)}) fusion(f32[1024,768]{1,0:T(8,128)} %fusion.83, f32[768]{0:T(1024)} %param.43, bf16[1024,768]{1,0:T(8,128)(2,1)} %all-gather.15.cloned.1.call-done, bf16[768,768]{0,1:T(8,128)(2,1)} %all-gather.13.cloned.1.call-done), kind=kOutput, calls=%fused_computation.23 | convolution fusion | flops 1229192448 | bytes 7477248 | tf_op jit(solution)/shard_map/dot_general | solution.py:22
  255.9 1.2 copy-done.58
  257.1 2.6 convolution_convert_fusion.1
  259.7 5.5 convolution_convert_fusion.2
  265.3 22.7 %reduce-scatter.15.cloned.1.call-done = bf16[256,768]{1,0:T(8,128)(2,1)} async-done(((bf16[1024,768]{1,0:T(8,128)(2,1)}), bf16[256,768]{1,0:T(8,128)(2,1)}) %reduce-scatter.15.cloned.1.call-update) | async-done | bytes 393232 | tf_op jit(solution)/shard_map/reduce_scatter | solution.py:55
  288.0 2.3 fusion.57
  291.4 27.2 %reduce-scatter.13.cloned.1.call-done = bf16[256,768]{1,0:T(8,128)(2,1)} async-done(((bf16[1024,768]{1,0:T(8,128)(2,1)}), bf16[256,768]{1,0:T(8,128)(2,1)}) %reduce-scatter.13.cloned.1.call-update) | async-done | bytes 393232 | tf_op jit(solution)/shard_map/reduce_scatter | solution.py:216
  318.6 3.3 fusion.74
  321.9 0.9 copy-done.3
  322.8 0.8 convert_element_type.165
  325.3 17.9 %all-gather.17.cloned.1.call-done = bf16[1024,768]{1,0:T(8,128)(2,1)} async-done(((bf16[256,768]{1,0:T(8,128)(2,1)}), bf16[1024,768]{1,0:T(8,128)(2,1)}) %all-gather.17.cloned.1.call-update) | async-done | bytes 1572880 | tf_op jit(solution)/shard_map/all_gather | solution.py:51
  343.2 2.2 convolution_convert_fusion.4
  346.8 0.9 multiply_convert_fusion.1
  350.1 1.9 multiply_reduce_fusion
  352.0 1.3 convert_reduce_fusion.5
  353.2 1.4 multiply_convert_fusion
  354.7 1.1 fusion.35
  357.4 2.6 convolution_convert_fusion
  360.0 1.6 convolution_bitcast_fusion
  361.7 5.6 fusion.72
  367.7 5.1 fusion.84
  373.0 2.4 fusion.68
  375.4 3.1 copy.64
  378.5 5.7 all-to-all-start.1
  384.2 4.0 reduce-scatter.17.cloned.1.call-done
  388.2 1.4 fusion.58
  389.7 2.1 fusion.51
  391.8 4.5 all-to-all-done.1
  396.3 3.6 all-to-all-start.3
  400.8 23.4 %all-reduce.3 = (f32[2,192]{1,0:T(2,128)}, f32[768]{0:T(1024)}) all-reduce(f32[2,192]{1,0:T(2,128)S(1)} %pad_maximum_fusion.4, f32[768]{0:T(1024)S(1)} %copy-done.52), channel_id=1, replica_groups=mesh['dp'=8,'tensor'=4] {'dp'}, use_global_device_ids=true, to_apply=%region_28.30 | all-reduce | flops 1152 | bytes 9216 | tf_op jit(solution)/shard_map/psum | solution.py:280
  424.3 30.8 %reduce-scatter.25.cloned.1.call-done = f32[96,192]{1,0:T(8,128)} async-done(((f32[768,192]{1,0:T(8,128)}), f32[96,192]{1,0:T(8,128)}) %reduce-scatter.25.cloned.1.call-update) | async-done | bytes 73744
  455.1 1.6 copy.70
  456.7 41.3 %all-reduce.2 = (f32[768]{0:T(1024)}, f32[768]{0:T(1024)}, f32[768]{0:T(1024)}, f32[768]{0:T(1024)}, f32[768]{0:T(1024)}, /*index=5*/f32[768]{0:T(1024)}) all-reduce(f32[768]{0:T(1024)S(1)} %get-tuple-element.83, f32[768]{0:T(1024)S(1)} %get-tuple-element.88, ...), channel_id=1, replica_groups=mesh['dp'=8,'tensor'=4] {'dp','tensor'}, use_global_device_ids=true, to_apply=%region_22.24 | all-reduce | flops 4608 | bytes 36864 | tf_op jit(solution)/shard_map/psum | solution.py:281
  498.6 1.0 broadcast_select_fusion
  499.6 28.4 %reduce-scatter.23.cloned.1.call-done = f32[768,96]{0,1:T(8,128)} async-done(((f32[768,768]{0,1:T(8,128)}), f32[768,96]{0,1:T(8,128)}) %reduce-scatter.23.cloned.1.call-update) | async-done | bytes 294928 | tf_op jit(solution)/shard_map/reduce_scatter | solution.py:277
  527.9 72.4 %reduce-scatter.21.cloned.1.call-done = f32[96,768]{1,0:T(8,128)} async-done(((f32[768,768]{1,0:T(8,128)}), f32[96,768]{1,0:T(8,128)}) %reduce-scatter.21.cloned.1.call-update) | async-done | bytes 294928 | tf_op jit(solution)/shard_map/reduce_scatter | solution.py:276
  600.3 72.5 %reduce-scatter.19.cloned.1.call-done = f32[96,3,192]{2,0,1:T(8,128)} async-done(((f32[768,3,192]{2,0,1:T(8,128)}), f32[96,3,192]{2,0,1:T(8,128)}) %reduce-scatter.19.cloned.1.call-update) | async-done | bytes 221200 | tf_op jit(solution)/shard_map/reduce_scatter | solution.py:274
  (200 shorter events, 16.4 us)
Async XLA Ops:
  8.0 23.6 %copy-start.38 = (f32[768]{0:T(1024)S(1)}, f32[768]{0:T(1024)}, u32[]{:S(2)}) copy-start(f32[768]{0:T(1024)} %param.34) | copy-start | bytes 9220
  8.0 23.6 %copy-start.51 = (f32[768]{0:T(1024)S(1)}, f32[768]{0:T(1024)}, u32[]{:S(2)}) copy-start(f32[768]{0:T(1024)} %param.35) | copy-start | bytes 9220
  8.1 24.6 %copy-start.53 = (s32[8,4]{0,1:T(4,128)S(1)}, s32[8,4]{0,1:T(4,128)}, u32[]{:S(2)}) copy-start(s32[8,4]{0,1:T(4,128)} %param.32) | copy-start | bytes 388
  8.1 25.0 %copy-start.34 = (f32[192,96]{1,0:T(8,128)S(1)}, f32[192,96]{1,0:T(8,128)}, u32[]{:S(2)}) copy-start(f32[192,96]{1,0:T(8,128)} %param.38) | copy-start | bytes 221188
  8.1 25.1 %copy-start.33 = (f32[96,3,192]{2,0,1:T(8,128)S(1)}, f32[96,3,192]{2,0,1:T(8,128)}, u32[]{:S(2)}) copy-start(f32[96,3,192]{2,0,1:T(8,128)} %param.36) | copy-start | bytes 663556
  8.1 97.5 %all-gather.7.cloned.1.call-start = ((), (), s32[]{:S(2)}) async-start(), calls=%async_computation.12 | async-start | bytes 1966080 | tf_op jit(solution)/shard_map/all_gather | solution.py:188
  31.5 38.7 %copy-start.42 = (f32[256]{0:T(256)}, f32[256]{0:T(256)S(1)}, u32[]{:S(2)}) copy-start(f32[256]{0:T(256)S(1)} %div.45) | copy-start | bytes 3076
  31.6 38.6 %copy-start.44 = (f32[256]{0:T(256)}, f32[256]{0:T(256)S(1)}, u32[]{:S(2)}) copy-start(f32[256]{0:T(256)S(1)} %add_rsqrt_fusion.1) | copy-start | bytes 3076
  32.6 70.7 %copy-start.54 = (f32[2,192]{1,0:T(2,128)S(1)}, f32[2,192]{1,0:T(2,128)}, u32[]{:S(2)}) copy-start(f32[2,192]{1,0:T(2,128)} %param.37) | copy-start | bytes 4612
  32.6 114.3 %reduce-scatter.11.cloned.1.call-start = ((), (), s32[]{:S(2)}) async-start(), calls=%async_computation.13 | async-start | bytes 1966080 | tf_op jit(solution)/shard_map/reduce_scatter | solution.py:208
  70.2 37.9 %copy-start.9 = (bf16[768,3,192]{0,2,1:T(8,128)(2,1)}, bf16[768,3,192]{0,2,1:T(8,128)(2,1)S(1)}, u32[]{:S(2)}) copy-start(bf16[768,3,192]{0,2,1:T(8,128)(2,1)S(1)} %copy.58) | copy-start | bytes 2654212
  108.1 1.8 copy-start.22
  108.2 2.9 copy-start.7
  108.3 6.1 copy-start.15
  108.4 2.7 copy-start.17
  108.4 1.9 copy-start.25
  112.9 2.7 copy-start.2
  112.9 2.7 copy-start.35
  114.4 2.8 copy-start.41
  115.5 2.5 copy-start.11
  117.2 29.7 %copy-start.36 = (f32[768]{0:T(1024)S(1)}, f32[768]{0:T(1024)}, u32[]{:S(2)}) copy-start(f32[768]{0:T(1024)} %param.39) | copy-start | bytes 9220
  117.2 31.6 %copy-start.37 = (f32[768]{0:T(1024)S(1)}, f32[768]{0:T(1024)}, u32[]{:S(2)}) copy-start(f32[768]{0:T(1024)} %param.40) | copy-start | bytes 9220
  119.8 51.5 %all-gather.11.cloned.1.call-start = ((), (), s32[]{:S(2)}) async-start(), calls=%async_computation.15 | async-start | bytes 1327104 | tf_op jit(solution)/shard_map/all_gather | solution.py:180
  121.6 63.9 %all-gather.9.cloned.1.call-start = ((), (), s32[]{:S(2)}) async-start(), calls=%async_computation.14 | async-start | bytes 1966080 | tf_op jit(solution)/shard_map/all_gather | solution.py:213
  150.8 78.5 %all-gather.13.cloned.1.call-start = ((), (), s32[]{:S(2)}) async-start(), calls=%async_computation.16 | async-start | bytes 1327104 | tf_op jit(solution)/shard_map/all_gather | solution.py:181
  152.5 96.5 %all-gather.15.cloned.1.call-start = ((), (), s32[]{:S(2)}) async-start(), calls=%async_computation.18 | async-start | bytes 1966080 | tf_op jit(solution)/shard_map/all_gather | solution.py:51
  171.1 116.9 %reduce-scatter.15.cloned.1.call-start = ((), (), s32[]{:S(2)}) async-start(), calls=%async_computation.19 | async-start | bytes 1966080 | tf_op jit(solution)/shard_map/reduce_scatter | solution.py:55
  249.0 8.1 %copy-start.55 = (bf16[768,768]{1,0:T(8,128)(2,1)S(1)}, bf16[768,768]{1,0:T(8,128)(2,1)}, u32[]{:S(2)}) copy-start(bf16[768,768]{1,0:T(8,128)(2,1)} %all-gather.11.cloned.1.call-done) | copy-start | bytes 3538948
  255.9 1.2 copy-start.58
  259.7 58.9 %reduce-scatter.13.cloned.1.call-start = ((), (), s32[]{:S(2)}) async-start(), calls=%async_computation.17 | async-start | bytes 1966080 | tf_op jit(solution)/shard_map/reduce_scatter | solution.py:216
  265.3 77.9 %all-gather.17.cloned.1.call-start = ((), (), s32[]{:S(2)}) async-start(), calls=%async_computation.20 | async-start | bytes 1966080 | tf_op jit(solution)/shard_map/all_gather | solution.py:51
  323.6 64.6 %reduce-scatter.17.cloned.1.call-start = ((), (), s32[]{:S(2)}) async-start(), calls=%async_computation.21 | async-start | bytes 1966080 | tf_op jit(solution)/shard_map/reduce_scatter | solution.py:55
  343.2 2.8 copy-start.26
  346.8 2.4 slice-start
  346.8 1.5 copy-start.21
  346.8 3.0 slice-start.1
  347.9 2.2 copy-start.16
  353.2 3.4 copy-start.29
  353.2 1.4 copy-start.8
  355.7 1.6 copy-start.10
  357.3 2.7 copy-start.6
  357.3 2.7 copy-start.13
  359.9 1.8 copy-start.56
  360.0 95.1 %reduce-scatter.25.cloned.1.call-start = ((), (), s32[]{:S(2)}) async-start(), calls=%async_computation.25 | async-start | bytes 884736
  361.7 166.3 %reduce-scatter.23.cloned.1.call-start = ((), (), s32[]{:S(2)}) async-start(), calls=%async_computation.24 | async-start | bytes 2654208 | tf_op jit(solution)/shard_map/reduce_scatter | solution.py:277
  367.4 5.6 copy-start.14
  367.4 5.6 copy-start.28
  367.4 5.6 copy-start.30
  367.4 5.6 copy-start.32
  367.4 232.9 %reduce-scatter.21.cloned.1.call-start = ((), (), s32[]{:S(2)}) async-start(), calls=%async_computation.23 | async-start | bytes 2654208 | tf_op jit(solution)/shard_map/reduce_scatter | solution.py:276
  372.9 299.9 %reduce-scatter.19.cloned.1.call-start = ((), (), s32[]{:S(2)}) async-start(), calls=%async_computation.22 | async-start | bytes 2654208 | tf_op jit(solution)/shard_map/reduce_scatter | solution.py:274
  375.4 12.8 %copy-start.39 = (f32[768]{0:T(1024)S(1)}, f32[768]{0:T(1024)}, u32[]{:S(2)}) copy-start(f32[768]{0:T(1024)} %param.34) | copy-start | bytes 9220
  375.4 12.8 %copy-start.43 = (f32[256]{0:T(256)S(1)}, f32[256]{0:T(256)}, u32[]{:S(2)}) copy-start(f32[256]{0:T(256)} %copy-done.42) | copy-start | bytes 3076
  375.4 12.8 %copy-start.45 = (f32[256]{0:T(256)S(1)}, f32[256]{0:T(256)}, u32[]{:S(2)}) copy-start(f32[256]{0:T(256)} %copy-done.44) | copy-start | bytes 3076
  375.4 14.3 %copy-start.4 = (f32[256,768]{1,0:T(8,128)S(1)}, f32[256,768]{1,0:T(8,128)}, u32[]{:S(2)}) copy-start(f32[256,768]{1,0:T(8,128)} %copy-done.3) | copy-start | bytes 2359300
  378.4 21.5 %copy-start.57 = (s32[8]{0:T(128)S(1)}, s32[8]{0:T(128)}, u32[]{:S(2)}) copy-start(s32[8]{0:T(128)} %param.33) | copy-start | bytes 100
  378.4 21.5 %copy-start.5 = (bf16[8,32,768]{2,1,0:T(8,128)(2,1)S(1)}, bf16[8,32,768]{2,1,0:T(8,128)(2,1)}, u32[]{:S(2)}) copy-start(bf16[8,32,768]{2,1,0:T(8,128)(2,1)} %all_to_all.34) | copy-start | bytes 1179652
  378.5 22.4 %copy-start.52 = (f32[768]{0:T(1024)S(1)}, f32[768]{0:T(1024)}, u32[]{:S(2)}) copy-start(f32[768]{0:T(1024)} %get-tuple-element.99) | copy-start | bytes 9220
  378.5 78.2 %copy-start.48 = (f32[768]{0:T(1024)S(1)}, f32[768]{0:T(1024)}, u32[]{:S(2)}) copy-start(f32[768]{0:T(1024)} %get-tuple-element.79) | copy-start | bytes 9220
  378.5 78.2 %copy-start.49 = (f32[768]{0:T(1024)S(1)}, f32[768]{0:T(1024)}, u32[]{:S(2)}) copy-start(f32[768]{0:T(1024)} %get-tuple-element.87) | copy-start | bytes 9220
  378.5 78.2 %copy-start.50 = (f32[768]{0:T(1024)S(1)}, f32[768]{0:T(1024)}, u32[]{:S(2)}) copy-start(f32[768]{0:T(1024)} %get-tuple-element.103) | copy-start | bytes 9220
  378.5 17.8 %all-to-all-start.1 = ((bf16[8,32,768]{2,1,0:T(8,128)(2,1)}), bf16[8,32,768]{2,1,0:T(8,128)(2,1)S(1)}, u32[]{:S(2)}, u32[]{:S(2)}) async-start(bf16[8,32,768]{2,1,0:T(8,128)(2,1)} %bitcast.15), calls=%async_computation.3 | async-start | bytes 786432 | tf_op jit(solution)/shard_map/all_to_all | solution.py:264
  389.6 283.2 %copy-start.1 = (bf16[256,768]{1,0:T(8,128)(2,1)S(1)}, bf16[256,768]{1,0:T(8,128)(2,1)}, u32[]{:S(2)}) copy-start(bf16[256,768]{1,0:T(8,128)(2,1)} %param.31) | copy-start | bytes 1179652
  396.3 101.7 %all-to-all-start.3 = ((bf16[8,32,768]{2,1,0:T(8,128)(2,1)}), bf16[8,32,768]{2,1,0:T(8,128)(2,1)S(1)}, u32[]{:S(2)}, u32[]{:S(2)}) async-start(bf16[8,32,768]{2,1,0:T(8,128)(2,1)} %bitcast.30), calls=%async_computation.7 | async-start | bytes 786432 | tf_op jit(solution)/shard_map/all_to_all | solution.py:265
  (13 other events, 11.0 us)
Sparse Core Ops, SparseCore 0:
  32.8 18.3 all-gather.6
  120.0 26.9 reduce-scatter.10
  259.8 28.1 reduce-scatter.14
  290.4 28.1 reduce-scatter.12
Sparse Core Ops, SparseCore 1:
  123.3 41.1 all-gather.10
  166.5 18.9 all-gather.8
  187.8 41.5 all-gather.12
  231.0 18.0 all-gather.14
  323.7 19.5 all-gather.16
  360.0 28.1 reduce-scatter.16
  391.3 63.7 reduce-scatter.24
  459.4 68.5 reduce-scatter.22
  532.3 68.0 reduce-scatter.20
  604.8 67.9 reduce-scatter.18
where the time goes:
time: 681 us; the launch traced here: 680 us
  waiting for transfers between devices  379 us (56%)
  blocking collectives  171 us (25%)
  matrix products  55.5 us (8%)
  other arithmetic  30.1 us (4%)
  local copies, waits for them, and re-layouts  17.6 us (3%)
  between operations  16.2 us (2%)
  starting transfers between devices  10.6 us (2%)
    reduce_scatter x1, waiting for transfers between devices, local(): lax.psum_scatter(qkv_grad, 'dp', scatter_dimension=0, tiled=True)  72.5 us
    reduce_scatter x1, waiting for transfers between devices, local(): lax.psum_scatter(fc_grad, 'dp', scatter_dimension=0, tiled=True)  72.4 us
    psum x1, blocking collectives, local(): lax.psum((ln1_gain_grad, ln1_bias_grad, attn_out_bias_grad, ln2_gain_grad...  41.3 us
    all_gather x1, waiting for transfers between devices, local(): lax.all_gather(proj_weight.astype(jnp.bfloat16), 'dp', axis=1, tiled=True)  39 us
    all_gather x2, waiting for transfers between devices, grad_rows(): return lax.all_gather(local_rows, 'tensor', axis=0, tiled=True)  37.6 us
    all_gather x1, blocking collectives, local(): lax.all_gather(qkv_weight.astype(jnp.bfloat16), 'dp', axis=0, tiled=True)  36 us
    all_gather x1, blocking collectives, local(): lax.all_gather(attn_out_weight.astype(jnp.bfloat16), 'dp', axis=1, tiled=...  33 us
    unnamed x15, waiting for transfers between devices  31 us
  transfers between devices with their start and end apart: 16, of which 13 were waited for; matrix products, arithmetic and copies ran while one was open for 7% of the time, Pallas kernels for 0%

commit v1 on v0

v1 whole, which is shorter than its diff:
```python
import functools

import jax
import jax.numpy as jnp
from jax import lax
from jax.experimental import pallas as pl
from jax.experimental.pallas import tpu as pltpu
from jax.sharding import Mesh
from jax.sharding import PartitionSpec as P

HEAD_DIM = 64
EPSILON = 1e-05
MASKED = -1e30
BF = jnp.bfloat16
F32 = jnp.float32
MESH = pl.DeviceIdType.MESH
CURVE = 0.7978845608028654
CUBE = 0.044715

CHUNKS = 2
STEP = 32

QKV, OUT, FC, PROJ = "wqkv", "wo", "w1", "w2"
H1, GF, H2, DR = "h1", "gf", "h2", "dr"

NN = ((1,), (0,))
NT = ((1,), (1,))
TN = ((0,), (0,))


class Refs(dict):
    __getattr__ = dict.__getitem__


def dot(left_side, right_side, form):
    return lax.dot_general(
        left_side, right_side, (form, ((), ())), preferred_element_type=F32
    )


def kernel(cfg, *refs):
    (n, packs, L, S, D, HC, FH, inside) = cfg
    names = cfg_names(cfg)
    r = Refs(zip(names, refs))
    slabs, hslabs = (r.slab0, r.slab1), (r.hslab0, r.hslab1)
    backs = (r.back0, r.back1) if inside else None
    NH = HC // HEAD_DIM
    NZ = n // 2
    WR = D // n
    PR = L // n
    CR = L // CHUNKS
    B = L

    hi = lax.axis_index("hi")
    lo = lax.axis_index("lo")
    t = lax.axis_index("tensor")
    z, xx = hi // 2, hi % 2
    y, c = t // 2, t % 2
    dev = lambda h, tt: (h, lo, tt)
    mate = dev(hi, 2 * y + 1 - c)
    ynb = dev(hi, 2 * (1 - y) + c)
    ymate = dev(hi, 2 * (1 - y) + 1 - c)
    xnb = dev(2 * z + 1 - xx, t)

    def zdev(k):
        return dev(2 * ((z + k) % NZ) + xx, t)

    def block_of(k):
        return 2 * ((y + k // 2) % 2) + (c + k % 2) % 2

    def rows(start, size, mult=None):
        return pl.ds(pl.multiple_of(start, mult or size), size)

    def block_rows(k):
        return rows(block_of(k) * B, B)

    def rcopy(src, dst, send, recv, target):
        return pltpu.make_async_remote_copy(
            src_ref=src,
            dst_ref=dst,
            send_sem=send,
            recv_sem=recv,
            device_id=target,
            device_id_type=MESH,
        )

    barrier = pltpu.get_barrier_semaphore()
    peers = [dev((hi + k) % n, t) for k in range(1, n)] + [mate, ynb, ymate]
    for peer in peers:
        pl.semaphore_signal(barrier, inc=1, device_id=peer, device_id_type=MESH)

    def a2a(tag, k, source, target):
        sem = r.a2a_sem
        to = (hi + k) % n
        return rcopy(source(to), target(hi), sem.at[0, tag, k - 1], sem.at[1, tag, k - 1], dev(to, t))

    def a2a_in_copy(tag, k):
        return a2a(
            tag,
            k,
            lambda to: r.sent.at[tag, to],
            lambda me: r.came.at[tag, rows(me * PR, PR)],
        )

    def a2a_out_copy(tag, k):
        return a2a(
            2 + tag,
            k,
            lambda to: r.made.at[tag, rows(to * PR, PR)],
            lambda me: backs[tag].at[me],
        )

    def pick_pieces(tag, source):
        def one(k, _):
            where = jnp.int32(0)
            for j in range(n):
                where = jnp.where(r.order[j] == k, j, where)
            r.sent[tag, k] = source[where]
            return 0

        lax.fori_loop(0, n, one, 0)
        r.came[tag, rows(hi * PR, PR)] = r.sent[tag, hi]

    if inside:
        pick_pieces(0, r.x)
    pl.semaphore_wait(barrier, len(peers))
    if inside:
        for k in range(1, n):
            a2a_in_copy(0, k).start()
        pick_pieces(1, r.g)
    else:
        r.came[0] = r.x[...]
        r.came[1] = r.g[...]

    WG = (QKV, OUT, FC, PROJ)

    def wslot(name, ref, slot):
        where = rows(slot * WR, WR, 16)
        return ref.at[:, where] if name == QKV else ref.at[where]

    def wg_z(name, k):
        sem = r.wg_sem
        a = WG.index(name)
        own = wslot(name, r[name], hi)
        return rcopy(own, own, sem.at[0, a, k], sem.at[1, a, k], zdev(k))

    def wg_x(name, k):
        sem = r.wg_sem
        a = WG.index(name)
        slot = wslot(name, r[name], 2 * ((z - k + NZ) % NZ) + xx)
        return rcopy(slot, slot, sem.at[0, a, NZ + k], sem.at[1, a, NZ + k], xnb)

    def wg_start(name):
        for k in range(1, NZ):
            wg_z(name, k).start()
        wg_x(name, 0).start()

    def wg_forward(name):
        for k in range(1, NZ):
            wg_z(name, k).wait_recv()
            wg_x(name, k).start()

    def wg_wait(name):
        for k in range(NZ):
            wg_x(name, k).wait_recv()

    def wg_drain(name):
        for k in range(1, NZ):
            wg_z(name, k).wait_send()
        for k in range(NZ):
            wg_x(name, k).wait_send()

    own_w = rows(hi * WR, WR, 16)
    for i in range(3):
        r.wqkv[i, own_w] = r.qkv_in[:, i, :].astype(BF)
    r.w1[own_w] = r.fc_in[...].astype(BF)
    r.turn[...] = jnp.zeros_like(r.turn)
    r.turn[:, :WR] = r.proj_in[...].astype(F32)
    for i in range(FH // 256):
        r.w2[own_w, i * 256 : (i + 1) * 256] = r.turn[i * 256 : (i + 1) * 256].T[:WR].astype(BF)
    r.turn[:HC, :WR] = r.out_in[...].astype(F32)
    r.wo[own_w] = r.turn[:256].T[:WR, :HC].astype(BF)

    AG = (H1, GF, H2, DR)

    def ag(name, kind, ch):
        sem = r.ag_sem
        a = AG.index(name)
        full = r[name]
        if kind == 2:
            where = rows(block_of(2) * B + ch * CR, CR)
        else:
            where = rows(t * B + ch * CR, CR)
        target = ynb if kind == 0 else mate
        part = full.at[where]
        return rcopy(part, part, sem.at[0, a, kind, ch], sem.at[1, a, kind, ch], target)

    def ag_send(name, ch):
        ag(name, 0, ch).start()
        ag(name, 1, ch).start()

    def ag_forward(name, ch):
        ag(name, 0, ch).wait_recv()
        ag(name, 2, ch).start()

    def ag_arrive(name, k):
        for ch in range(CHUNKS):
            if k == 1:
                ag(name, 1, ch).wait_recv()
            elif k == 2:
                ag_forward(name, ch)
            else:
                ag(name, 2, ch).wait_recv()

    def ag_drain(name):
        for kind in range(3):
            for ch in range(CHUNKS):
                ag(name, kind, ch).wait_send()

    def rs_bufs(tag):
        if tag == 3:
            return r.msy, r.mry, r.keepy, r.ysy, r.yry
        return r.msc, r.mrc, r.keepc, r.ysc, r.yrc

    def rs_m(tag, i):
        ms, mr, _, _, _ = rs_bufs(tag)
        sem = r.rs_sem
        return rcopy(ms.at[i], mr.at[i], sem.at[0, tag, i], sem.at[1, tag, i], mate)

    def rs_y(tag, ch):
        _, _, _, ys, yr = rs_bufs(tag)
        sem = r.rs_sem
        where = pl.ds(ch * CR, CR)
        return rcopy(ys.at[where], yr.at[where], sem.at[0, tag, 2 + ch], sem.at[1, tag, 2 + ch], ynb)

    def rs_put(tag, k, value, at=None):
        ms, _, keep, _, _ = rs_bufs(tag)
        where = slice(None) if at is None else at
        i = 0 if k >= 2 else 1
        if k % 2:
            ms[i, where] = value.astype(BF)
        else:
            keep[i, where] = value

    def rs_ship(tag):
        _, mr, keep, ys, _ = rs_bufs(tag)
        rs_m(tag, 0).wait_recv()
        for ch in range(CHUNKS):

            def one(s, _):
                at = rows(ch * CR + s * STEP, STEP)
                ys[at] = (keep[0, at] + mr[0, at].astype(F32)).astype(BF)
                return 0

            lax.fori_loop(0, CR // STEP, one, 0)
            rs_y(tag, ch).start()

    def rs_total(tag, at):
        _, mr, keep, _, yr = rs_bufs(tag)
        return keep[1, at] + mr[1, at].astype(F32) + yr[at].astype(F32)

    def rs_drain(tag):
        for i in range(2):
            rs_m(tag, i).wait_send()
        for ch in range(CHUNKS):
            rs_y(tag, ch).wait_send()

    GR = {name: "g" + name for name in WG}

    def gr_x(name, k):
        sem = r.gr_sem
        a = WG.index(name)
        slot = wslot(name, r[GR[name]], 2 * k + 1 - xx)
        return rcopy(slot, r[name + "_xr"].at[k], sem.at[0, a, k], sem.at[1, a, k], xnb)

    def gr_z(name, k):
        sem = r.gr_sem
        a = WG.index(name)
        return rcopy(
            r[name + "_zs"].at[k - 1],
            r[name + "_zr"].at[k - 1],
            sem.at[0, a, NZ + k],
            sem.at[1, a, NZ + k],
            zdev(k),
        )

    def gr_start(name):
        for k in range(NZ):
            gr_x(name, k).start()

    def gr_mid(name):
        for k in range(NZ):
            gr_x(name, k).wait_recv()
        for k in range(1, NZ):
            to = (z + k) % NZ
            mine = wslot(name, r[GR[name]], 2 * to + xx)[...].astype(F32)
            r[name + "_zs"][k - 1] = (mine + r[name + "_xr"][to].astype(F32)).astype(BF)
            gr_z(name, k).start()

    def gr_finish(name):
        total = wslot(name, r[GR[name]], hi)[...].astype(F32) + r[name + "_xr"][z].astype(F32)
        for k in range(1, NZ):
            gr_z(name, k).wait_recv()
            total = total + r[name + "_zr"][k - 1].astype(F32)
        return total

    def gr_drain(name):
        for k in range(NZ):
            gr_x(name, k).wait_send()
        for k in range(1, NZ):
            gr_z(name, k).wait_send()

    tpeers = [mate, ynb, ymate]
    SHARED = (24, 16)

    def sm_t(tag, i):
        sem = r.sm_sem
        part = slabs[tag].at[t]
        return rcopy(part, part, sem.at[0, tag, i], sem.at[1, tag, i], tpeers[i])

    def sm_h(tag, k):
        sem = r.sm_sem
        part = hslabs[tag].at[hi]
        return rcopy(part, part, sem.at[0, tag, 3 + k], sem.at[1, tag, 3 + k], dev((hi + k) % n, t))

    def spread(tag, at, value):
        for j in range(value.shape[1] // 128):
            slabs[tag][t, at + j : at + j + 1] = value[:, j * 128 : (j + 1) * 128]

    def sm_start(tag):
        for i in range(3):
            sm_t(tag, i).start()

    def sm_mid(tag):
        for i in range(3):
            sm_t(tag, i).wait_recv()
        slab, hslab = slabs[tag], hslabs[tag]
        total = slab[0]
        for i in range(1, 4):
            total = total + slab[i]
        if tag == 0:
            keep = lax.broadcasted_iota(jnp.int32, total.shape, 0) < SHARED[0]
            total = jnp.where(keep, total, slab[t])
        hslab[hi] = total
        for k in range(1, n):
            sm_h(tag, k).start()

    def sm_finish(tag):
        for k in range(1, n):
            sm_h(tag, k).wait_recv()
        hslab = hslabs[tag]
        total = hslab[0]
        for k in range(1, n):
            total = total + hslab[k]
        return total

    def sm_drain(tag):
        for i in range(3):
            sm_t(tag, i).wait_send()
        for k in range(1, n):
            sm_h(tag, k).wait_send()

    def fold(value):
        return jnp.sum(value.reshape(value.shape[0] // 8, 8, value.shape[1]), axis=0)

    for slab in slabs:
        slab[t] = jnp.zeros(slab.shape[1:], F32)
    r.acc[...] = jnp.zeros_like(r.acc)
    r.acc_f[...] = jnp.zeros_like(r.acc_f)
    r.acc_h[...] = jnp.zeros_like(r.acc_h)

    if inside:
        for k in range(1, n):
            a2a_in_copy(0, k).wait_recv()
    wg_start(QKV)

    def norm_step(values, at, gain, bias, cen, scale):
        mean = jnp.mean(values, axis=1, keepdims=True)
        var = jnp.mean(values * values, axis=1, keepdims=True) - mean * mean
        inv = lax.rsqrt(var + EPSILON)
        centered = (values - mean) * inv
        cen[at] = centered
        scale[at] = inv
        return (centered * gain + bias).astype(BF)

    def norm_back(grad, at, gain, cen, scale, acc_at):
        centered = cen[at]
        r.acc[acc_at] += fold(grad * centered)
        r.acc[acc_at + 1] += fold(grad)
        scaled = grad * gain
        return scale[at] * (
            scaled
            - jnp.mean(scaled, axis=1, keepdims=True)
            - centered * jnp.mean(scaled * centered, axis=1, keepdims=True)
        )

    for ch in range(CHUNKS):

        def one(s, _):
            at = rows(ch * CR + s * STEP, STEP)
            values = r.came[0, at].astype(F32)
            r.h1[rows(t * B + ch * CR + s * STEP, STEP)] = norm_step(
                values, at, r.ln1g[...], r.ln1b[...], r.cen1, r.scale1
            )
            return 0

        lax.fori_loop(0, CR // STEP, one, 0)
        ag_send(H1, ch)

    if inside:
        for k in range(1, n):
            a2a_in_copy(1, k).start()
    wg_forward(QKV)
    wg_start(OUT)
    wg_start(FC)
    wg_wait(QKV)

    lane = lax.broadcasted_iota(jnp.int32, (1, HC), 1)

    def head_mask(h):
        return (lane >= h * HEAD_DIM) & (lane < (h + 1) * HEAD_DIM)

    def project(s, _):
        @pl.when(s == 1)
        def _():
            ag_arrive(H1, 1)

        @pl.when(s == 2)
        def _():
            ag_arrive(H1, 2)

        @pl.when(s == 3)
        def _():
            ag_arrive(H1, 3)

        b = block_of(s)
        at = rows(b * B, B)
        hidden = r.h1[at]
        q = dot(hidden, r.wqkv[0], NN) + r.qvb[0:1]
        q = (q.astype(BF).astype(F32) * HEAD_DIM ** (-0.5)).astype(BF)
        for h in range(NH):
            r.qm[b, h * B : (h + 1) * B] = jnp.where(head_mask(h), q, jnp.zeros_like(q))
        k = dot(hidden, r.wqkv[1], NN)
        r.k[at] = k.astype(BF)
        r.kt[:, at] = k.T.astype(BF)
        v = dot(hidden, r.wqkv[2], NN) + r.qvb[1:2]
        r.v[at] = v.astype(BF)
        r.vt[:, at] = v.T.astype(BF)
        return 0

    lax.fori_loop(0, 4, project, 0)

    if inside:
        for k in range(1, n):
            a2a_in_copy(1, k).wait_recv()

    def own_grad(s, _):
        at = rows(s * STEP, STEP)
        value = r.came[1, at]
        r.gf[rows(t * B + s * STEP, STEP)] = value
        r.acc[5] += fold(value.astype(F32))
        return 0

    lax.fori_loop(0, B // STEP, own_grad, 0)
    for ch in range(CHUNKS):
        ag_send(GF, ch)
    wg_forward(OUT)
    wg_start(PROJ)

    pack = hi * (packs // n) + lo

    def attend(i):
        pos = i * B + lax.broadcasted_iota(jnp.int32, (1, B), 1)
        first = jnp.zeros((1, B), jnp.int32)
        end = jnp.int32(0)
        for s in range(r.lengths.shape[1]):
            length = r.lengths[pack, s]
            end = end + length
            first = first + jnp.where(pos >= end, length, 0)

        def scores(j, peak):
            key_pos = j * B + lax.broadcasted_iota(jnp.int32, (B, B), 0)
            allowed = (key_pos >= first) & (key_pos <= pos)
            keys = r.k[rows(j * B, B)]
            peaks = []
            for h in range(NH):
                raw = dot(keys, r.qm[i, h * B : (h + 1) * B], NT)
                raw = jnp.where(allowed, raw, MASKED)
                r.score[j, :, h * B : (h + 1) * B] = raw
                peaks.append(jnp.max(raw, axis=0, keepdims=True))
            return jnp.maximum(peak, jnp.concatenate(peaks, axis=1))

        peak = lax.fori_loop(0, i + 1, scores, jnp.full((1, NH * B), MASKED, F32))
        r.att[...] = jnp.zeros_like(r.att)

        def weigh(j, total):
            totals = []
            for h in range(NH):
                cols = slice(h * B, (h + 1) * B)
                weight = jnp.exp(r.score[j, :, cols] - peak[:, cols])
                totals.append(jnp.sum(weight, axis=0, keepdims=True))
                low = weight.astype(BF)
                r.e[i, j, :, cols] = low
                part = slice(h * HEAD_DIM, (h + 1) * HEAD_DIM)
                r.att[part] += dot(r.vt[part, rows(j * B, B)], low, NN)
            return total + jnp.concatenate(totals, axis=1)

        total = lax.fori_loop(0, i + 1, weigh, jnp.zeros((1, NH * B), F32))
        inverse = 1.0 / total
        for h in range(NH):
            part = slice(h * HEAD_DIM, (h + 1) * HEAD_DIM)
            own = inverse[:, h * B : (h + 1) * B]
            r.att[part] = r.att[part] * own
            r.inv[i, h : h + 1] = own
        out = r.att[...].T
        at = rows(i * B, B)
        r.a[at] = out
        r.al[at] = out.astype(BF)

    def attend_step(s, _):
        k = 3 - s
        i = block_of(k)
        attend(i)

        @pl.when(s == 0)
        def _():
            wg_wait(OUT)

        part = dot(r.al[rows(i * B, B)], r.wo[...], NT)

        @pl.when(s == 0)
        def _():
            rs_put(0, 3, part)
            rs_m(0, 0).start()

        @pl.when(s == 1)
        def _():
            rs_put(0, 2, part)
            rs_ship(0)

        @pl.when(s == 2)
        def _():
            rs_put(0, 1, part)
            rs_m(0, 1).start()

        @pl.when(s == 3)
        def _():
            rs_put(0, 0, part)

        return 0

    lax.fori_loop(0, 4, attend_step, 0)
    wg_forward(FC)

    rs_m(0, 1).wait_recv()
    for ch in range(CHUNKS):
        rs_y(0, ch).wait_recv()

        def one(s, _):
            at = rows(ch * CR + s * STEP, STEP)
            values = r.came[0, at].astype(F32) + rs_total(0, at) + r.aob[...]
            r.res[at] = values
            r.h2[rows(t * B + ch * CR + s * STEP, STEP)] = norm_step(
                values, at, r.ln2g[...], r.ln2b[...], r.cen2, r.scale2
            )
            return 0

        lax.fori_loop(0, CR // STEP, one, 0)
        ag_send(H2, ch)
    rs_drain(0)
    ag_arrive(GF, 1)
    ag_arrive(GF, 2)
    wg_forward(PROJ)
    ag_arrive(GF, 3)
    wg_wait(FC)
    wg_wait(PROJ)

    def feed(s, _):
        @pl.when(s == 1)
        def _():
            ag_arrive(H2, 1)

        @pl.when(s == 2)
        def _():
            ag_arrive(H2, 2)

        @pl.when(s == 3)
        def _():
            ag_arrive(H2, 3)

        at = block_rows(s)
        hidden = r.h2[at]
        grad = r.gf[at]
        for j in range(FH // 256):
            cols = slice(j * 256, (j + 1) * 256)
            u = dot(hidden, r.w1[:, cols], NN) + r.fcb[:, cols]
            dz = dot(grad, r.w2[:, cols], NN)
            square = u * u
            half = 0.5 + 0.5 * jnp.tanh(u * (CURVE + (CURVE * CUBE) * square))
            act = u * half
            r.zz[at, cols] = act.astype(BF)
            slope = half + act * (1.0 - half) * (2.0 * CURVE + (6.0 * CURVE * CUBE) * square)
            low = (dz * slope).astype(BF)
            r.du[at, cols] = low
            r.acc_f[:, cols] += fold(low.astype(F32))
        part = dot(r.du[at], r.w1[...], NT)

        @pl.when(s == 0)
        def _():
            rs_put(1, 0, part)

        @pl.when(s == 1)
        def _():
            rs_put(1, 1, part)
            rs_m(1, 1).start()

        @pl.when(s == 2)
        def _():
            rs_put(1, 2, part)

        @pl.when(s == 3)
        def _():
            rs_put(1, 3, part)
            rs_m(1, 0).start()

        return 0

    lax.fori_loop(0, 4, feed, 0)
    rs_ship(1)

    def grad_tiles(left, right, out, form=TN):
        def one(i, _):
            at = rows(i * 256, 256)
            out[at] = dot(left[:, at], right[...], form).astype(BF)
            return 0

        lax.fori_loop(0, D // 256, one, 0)

    grad_tiles(r.gf, r.zz, r.gw2)
    gr_start(PROJ)
    grad_tiles(r.h2, r.du, r.gw1)
    gr_start(FC)

    rs_m(1, 1).wait_recv()
    for ch in range(CHUNKS):
        rs_y(1, ch).wait_recv()

        def one(s, _):
            at = rows(ch * CR + s * STEP, STEP)
            back = norm_back(rs_total(1, at), at, r.ln2g[...], r.cen2, r.scale2, 2)
            grad = r.came[1, at].astype(F32) + back
            r.dres[at] = grad
            r.acc[4] += fold(grad)
            r.dr[rows(t * B + ch * CR + s * STEP, STEP)] = grad.astype(BF)
            return 0

        lax.fori_loop(0, CR // STEP, one, 0)
        ag_send(DR, ch)
    rs_drain(1)

    def upper(s, _):
        k = 3 - s
        part = dot(r.zz[block_rows(k)], r.w2[...], NT)

        @pl.when(s == 0)
        def _():
            rs_put(3, 3, part)
            rs_m(3, 0).start()

        @pl.when(s == 1)
        def _():
            rs_put(3, 2, part)

        @pl.when(s == 2)
        def _():
            rs_put(3, 1, part)
            rs_m(3, 1).start()

        @pl.when(s == 3)
        def _():
            rs_put(3, 0, part)

        return 0

    lax.fori_loop(0, 4, upper, 0)
    gr_mid(PROJ)
    gr_mid(FC)

    r.dk[...] = jnp.zeros_like(r.dk)
    r.dv[...] = jnp.zeros_like(r.dv)

    def attend_back(s, _):
        @pl.when(s == 1)
        def _():
            ag_arrive(DR, 1)

        @pl.when(s == 2)
        def _():
            ag_arrive(DR, 2)
            rs_ship(3)

        @pl.when(s == 3)
        def _():
            ag_arrive(DR, 3)

        i = block_of(s)
        at = rows(i * B, B)
        da = dot(r.dr[at], r.wo[...], NN).astype(BF).astype(F32)
        by_row = r.inv[i].T
        scale = by_row[:, NH - 1 : NH]
        for h in range(NH - 1):
            scale = jnp.where(head_mask(h), by_row[:, h : h + 1], scale)
        low = (da * scale).astype(BF)
        for h in range(NH):
            r.dam[h * B : (h + 1) * B] = jnp.where(head_mask(h), low, jnp.zeros_like(low))
        lined = (low.astype(F32) * r.a[at]).T
        deltas = [
            jnp.sum(lined[h * HEAD_DIM : (h + 1) * HEAD_DIM], axis=0, keepdims=True)
            for h in range(NH)
        ]
        r.att[...] = jnp.zeros_like(r.att)

        def over_keys(j, _):
            kr = rows(j * B, B)
            values = r.v[kr]
            for h in range(NH):
                cols = slice(h * B, (h + 1) * B)
                dp = dot(values, r.dam[cols], NT)
                ds = (r.e[i, j, :, cols].astype(F32) * (dp - deltas[h])).astype(BF)
                r.ds[:, cols] = ds
                part = slice(h * HEAD_DIM, (h + 1) * HEAD_DIM)
                r.att[part] += dot(r.kt[part, kr], ds, NN)
            r.dk[kr] += dot(r.ds[...], r.qm[i], NN)
            r.dv[kr] += dot(r.e[i, j], r.dam[...], NN)
            return 0

        lax.fori_loop(0, i + 1, over_keys, 0)
        dq = (r.att[...].T * HEAD_DIM ** (-0.5)).astype(BF)
        r.dqkv[0, at] = dq
        return 0

    lax.fori_loop(0, 4, attend_back, 0)

    def round_kv(b, _):
        at = rows(b * B, B)
        dv = r.dv[at].astype(BF)
        r.dqkv[1, at] = r.dk[at].astype(BF)
        r.dqkv[2, at] = dv
        r.acc_h[0] += fold(r.dqkv[0, at].astype(F32))
        r.acc_h[1] += fold(dv.astype(F32))
        return 0

    lax.fori_loop(0, 4, round_kv, 0)

    def lower(s, _):
        k = 3 - s
        at = block_rows(k)
        part = dot(r.dqkv[0, at], r.wqkv[0], NT)
        part = part + dot(r.dqkv[1, at], r.wqkv[1], NT)
        part = part + dot(r.dqkv[2, at], r.wqkv[2], NT)

        @pl.when(s == 0)
        def _():
            rs_put(2, 3, part)
            rs_m(2, 0).start()

        @pl.when(s == 1)
        def _():
            rs_put(2, 2, part)
            rs_ship(2)

        @pl.when(s == 2)
        def _():
            rs_put(2, 1, part)
            rs_m(2, 1).start()

        @pl.when(s == 3)
        def _():
            rs_put(2, 0, part)

        return 0

    lax.fori_loop(0, 4, lower, 0)

    def grad_qkv(i, _):
        at = rows(i * 256, 256)
        left = r.h1[:, at]
        for j in range(3):
            r.gwqkv[j, at] = dot(left, r.dqkv[j], TN).astype(BF)
        return 0

    lax.fori_loop(0, D // 256, grad_qkv, 0)
    gr_start(QKV)
    grad_tiles(r.dr, r.al, r.gwo)
    gr_start(OUT)

    rs_m(3, 1).wait_recv()
    for ch in range(CHUNKS):
        rs_y(3, ch).wait_recv()

    def finish_up(s, _):
        at = rows(s * STEP, STEP)
        r.made[0, at] = (r.res[at] + rs_total(3, at) + r.pjb[...]).astype(BF)
        return 0

    lax.fori_loop(0, B // STEP, finish_up, 0)
    if inside:
        for k in range(1, n):
            a2a_out_copy(0, k).start()
        r.back0[hi] = r.made[0, rows(hi * PR, PR)]
    else:
        r.out_y[...] = r.made[0]

    def line(value):
        return jnp.sum(value, axis=0, keepdims=True)

    for j, at in enumerate((5, 2, 3, 4)):
        spread(0, 6 * j, line(r.acc[at]))
    spread(0, 24, line(r.acc_f[...]))
    pad = jnp.zeros((1, 256 - HC), F32)
    for j in range(2):
        spread(0, 30 + 2 * j, jnp.concatenate([line(r.acc_h[j]), pad], axis=1))
    sm_start(0)

    rs_m(2, 1).wait_recv()
    for ch in range(CHUNKS):
        rs_y(2, ch).wait_recv()

        def one(s, _):
            at = rows(ch * CR + s * STEP, STEP)
            back = norm_back(rs_total(2, at), at, r.ln1g[...], r.cen1, r.scale1, 0)
            r.made[1, at] = (r.dres[at] + back).astype(BF)
            return 0

        lax.fori_loop(0, CR // STEP, one, 0)
    rs_drain(2)
    rs_drain(3)
    if inside:
        for k in range(1, n):
            a2a_out_copy(1, k).start()
        r.back1[hi] = r.made[1, rows(hi * PR, PR)]
    else:
        r.out_x[...] = r.made[1]
    for j in range(2):
        spread(1, 6 * j, line(r.acc[j]))
    sm_start(1)
    sm_mid(0)
    gr_mid(QKV)
    gr_mid(OUT)
    sm_mid(1)

    r.out_w2[...] = gr_finish(PROJ)
    r.out_w1[...] = gr_finish(FC)

    def put_back(tag, out):
        for k in range(1, n):
            a2a_out_copy(tag, k).wait_recv()

        def one(j, _):
            out[j] = backs[tag][r.order[j]]
            return 0

        lax.fori_loop(0, n, one, 0)

    if inside:
        put_back(0, r.out_y)
    r.out_early[...] = sm_finish(0)
    r.out_qkv[...] = gr_finish(QKV)
    r.out_wo[...] = gr_finish(OUT)
    r.out_late[...] = sm_finish(1)
    if inside:
        put_back(1, r.out_x)

    for name in WG:
        wg_drain(name)
        gr_drain(name)
    for name in AG:
        ag_drain(name)
    for tag in range(2):
        sm_drain(tag)
        if inside:
            for k in range(1, n):
                a2a_in_copy(tag, k).wait_send()
                a2a_out_copy(tag, k).wait_send()


def inputs():
    vmem = pl.BlockSpec(memory_space=pltpu.VMEM)
    smem = pl.BlockSpec(memory_space=pltpu.SMEM)
    return Refs(
        order=smem,
        lengths=smem,
        x=vmem,
        g=vmem,
        ln1g=vmem,
        ln1b=vmem,
        qkv_in=vmem,
        qvb=vmem,
        out_in=vmem,
        aob=vmem,
        ln2g=vmem,
        ln2b=vmem,
        fc_in=vmem,
        fcb=vmem,
        proj_in=vmem,
        pjb=vmem,
    )


def outputs(cfg):
    (n, packs, L, S, D, HC, FH, inside) = cfg
    WR = D // n
    tokens = (n, L // n, D) if inside else (L, D)
    return Refs(
        out_y=(tokens, BF),
        out_x=(tokens, BF),
        out_qkv=((3, WR, HC), F32),
        out_wo=((WR, HC), F32),
        out_w1=((WR, FH), F32),
        out_w2=((WR, FH), F32),
        out_early=((40, 128), F32),
        out_late=((16, 128), F32),
    )


def scratch(cfg):
    (n, packs, L, S, D, HC, FH, inside) = cfg
    NH = HC // HEAD_DIM
    NZ = n // 2
    WR = D // n
    V = pltpu.VMEM
    sem = pltpu.SemaphoreType.DMA
    blocks = S // L
    made = Refs(
        came=V((2, L, D), BF),
        made=V((2, L, D), BF),
        wqkv=V((3, D, HC), BF),
        wo=V((D, HC), BF),
        w1=V((D, FH), BF),
        w2=V((D, FH), BF),
        turn=V((FH, 128), F32),
        h1=V((S, D), BF),
        gf=V((S, D), BF),
        h2=V((S, D), BF),
        dr=V((S, D), BF),
        cen1=V((L, D), F32),
        cen2=V((L, D), F32),
        scale1=V((L, 1), F32),
        scale2=V((L, 1), F32),
        res=V((L, D), F32),
        dres=V((L, D), F32),
        qm=V((blocks, NH * L, HC), BF),
        k=V((S, HC), BF),
        v=V((S, HC), BF),
        kt=V((HC, S), BF),
        vt=V((HC, S), BF),
        score=V((blocks, L, NH * L), F32),
        e=V((blocks, blocks, L, NH * L), BF),
        att=V((HC, L), F32),
        inv=V((blocks, 8, L), F32),
        a=V((S, HC), F32),
        al=V((S, HC), BF),
        dam=V((NH * L, HC), BF),
        ds=V((L, NH * L), BF),
        dk=V((S, HC), F32),
        dv=V((S, HC), F32),
        dqkv=V((3, S, HC), BF),
        zz=V((S, FH), BF),
        du=V((S, FH), BF),
        acc=V((6, 8, D), F32),
        acc_f=V((8, FH), F32),
        acc_h=V((2, 8, HC), F32),
        slab0=V((4, 40, 128), F32),
        slab1=V((4, 16, 128), F32),
        hslab0=V((n, 40, 128), F32),
        hslab1=V((n, 16, 128), F32),
    )
    if inside:
        made.update(
            sent=V((2, n, L // n, D), BF),
            back0=V((n, L // n, D), BF),
            back1=V((n, L // n, D), BF),
            a2a_sem=sem((2, 4, n - 1)),
        )
    for late in "cy":
        made["ms" + late] = V((2, L, D), BF)
        made["mr" + late] = V((2, L, D), BF)
        made["keep" + late] = V((2, L, D), F32)
        made["ys" + late] = V((L, D), BF)
        made["yr" + late] = V((L, D), BF)
    for name, slot in ((QKV, (3, WR, HC)), (OUT, (WR, HC)), (FC, (WR, FH)), (PROJ, (WR, FH))):
        made["g" + name] = V(slot[:-2] + (D, slot[-1]), BF)
        made[name + "_xr"] = V((NZ,) + slot, BF)
        made[name + "_zs"] = V((NZ - 1,) + slot, BF)
        made[name + "_zr"] = V((NZ - 1,) + slot, BF)
    made.update(
        wg_sem=sem((2, 4, 2 * NZ)),
        gr_sem=sem((2, 4, 2 * NZ)),
        ag_sem=sem((2, 4, 3, CHUNKS)),
        rs_sem=sem((2, 4, 2 + CHUNKS)),
        sm_sem=sem((2, 2, 3 + n)),
    )
    return made


def cfg_names(cfg):
    return tuple(inputs()) + tuple(outputs(cfg)) + tuple(scratch(cfg))


def local(
    n,
    block_input,
    out_cotangent,
    seq_lengths,
    pack_order,
    ln1_gain,
    ln1_bias,
    qkv_weight,
    qv_bias,
    attn_out_weight,
    attn_out_bias,
    ln2_gain,
    ln2_bias,
    fc_weight,
    fc_bias,
    proj_weight,
    proj_bias,
):
    L, D = block_input.shape
    packs = pack_order.shape[0]
    HC = qv_bias.shape[1]
    FH = fc_bias.shape[0]
    S = L * lax.axis_size("tensor")
    outer = packs // n
    inside = outer == 1
    cfg = (n, packs, L, S, D, HC, FH, inside)
    tokens = (block_input, out_cotangent)
    weights = (qkv_weight, attn_out_weight, fc_weight, proj_weight)
    if inside:
        tokens = [v.reshape(n, L // n, D) for v in tokens]
    else:
        slots = jnp.arange(packs, dtype=jnp.int32)
        chosen = (pack_order[None, :] == slots[:, None]).astype(BF)

        def pick(which, v):
            return (
                jnp.dot(which, v.reshape(packs, -1), preferred_element_type=F32)
                .astype(BF)
                .reshape(L, D)
            )

        tokens = [
            lax.all_to_all(
                pick(chosen, v), ("hi", "lo"), split_axis=0, concat_axis=0, tiled=True
            )
            for v in tokens
        ]
        weights = [
            lax.all_gather(w.astype(BF), "lo", axis=axis, tiled=True)
            for w, axis in zip(weights, (0, 1, 0, 1))
        ]
    row = lambda v: v.reshape(1, -1)
    outs = outputs(cfg)
    made = pl.pallas_call(
        functools.partial(kernel, cfg),
        out_shape=[jax.ShapeDtypeStruct(shape, kind) for shape, kind in outs.values()],
        in_specs=list(inputs().values()),
        out_specs=[pl.BlockSpec(memory_space=pltpu.VMEM)] * len(outs),
        scratch_shapes=list(scratch(cfg).values()),
        compiler_params=pltpu.CompilerParams(
            collective_id=0, has_side_effects=True, vmem_limit_bytes=63 * 2**20
        ),
    )(
        pack_order,
        seq_lengths,
        *tokens,
        row(ln1_gain),
        row(ln1_bias),
        weights[0],
        qv_bias,
        weights[1],
        row(attn_out_bias),
        row(ln2_gain),
        row(ln2_bias),
        weights[2],
        row(fc_bias),
        weights[3],
        row(proj_bias),
    )
    g = Refs(zip(outs, made))
    out_y, out_x = g.out_y, g.out_x
    qkv_sum = jnp.transpose(g.out_qkv, (1, 0, 2))
    out_sum = g.out_wo.T
    fc_sum = g.out_w1
    proj_sum = g.out_w2.T
    early, late = g.out_early, g.out_late
    if inside:
        out_y, out_x = out_y.reshape(L, D), out_x.reshape(L, D)
    else:
        out_y, out_x = [
            pick(
                chosen.T,
                lax.all_to_all(v, ("hi", "lo"), split_axis=0, concat_axis=0, tiled=True),
            )
            for v in (out_y, out_x)
        ]
        qkv_sum, out_sum, fc_sum, proj_sum = [
            lax.psum_scatter(w, "lo", scatter_dimension=axis, tiled=True)
            for w, axis in ((qkv_sum, 0), (out_sum, 1), (fc_sum, 0), (proj_sum, 1))
        ]
        early, late = lax.psum((early, late), "lo")
    vec = D // 128
    shared = [early[j * vec : (j + 1) * vec].reshape(D) for j in range(4)]
    fc_bias_sum = early[4 * vec : 4 * vec + FH // 128].reshape(FH)
    head = 4 * vec + FH // 128
    qv_sum = early[head : head + 4].reshape(2, 256)[:, :HC]
    return (
        out_y,
        out_x,
        late[:vec].reshape(D),
        late[vec : 2 * vec].reshape(D),
        qkv_sum,
        qv_sum,
        out_sum,
        shared[3],
        shared[1],
        shared[2],
        fc_sum,
        fc_bias_sum,
        proj_sum,
        shared[0],
    )


def solution(mesh):
    groups, members = mesh.shape["dp"], mesh.shape["tensor"]
    n = min(8, groups)
    cut = Mesh(mesh.devices.reshape(n, groups // n, members), ("hi", "lo", "tensor"))
    dp = ("hi", "lo")
    return jax.shard_map(
        functools.partial(local, n),
        mesh=cut,
        in_specs=(
            P(("hi", "lo", "tensor"), None),
            P(("hi", "lo", "tensor"), None),
            P(),
            P(),
            P(),
            P(),
            P(dp, None, "tensor"),
            P(None, "tensor"),
            P("tensor", dp),
            P(),
            P(),
            P(),
            P(dp, "tensor"),
            P("tensor"),
            P("tensor", dp),
            P(),
        ),
        out_specs=(
            P(("hi", "lo", "tensor"), None),
            P(("hi", "lo", "tensor"), None),
            P(),
            P(),
            P(dp, None, "tensor"),
            P(None, "tensor"),
            P("tensor", dp),
            P(),
            P(),
            P(),
            P(dp, "tensor"),
            P("tensor"),
            P("tensor", dp),
            P(),
        ),
        check_vma=False,
    )
```

time: 681 us -> 211 us (0.31)
  waiting for transfers between devices: 379 us -> 0 us
  Pallas kernels: 0 us -> 192 us
  blocking collectives: 171 us -> 0 us
  matrix products: 55.5 us -> 0 us
  other arithmetic: 30.1 us -> 0 us
  between operations: 16.2 us -> 0.69 us
  starting transfers between devices: 10.6 us -> 0 us
    reduce_scatter x7 -> x0, waiting for transfers between devices: 252 us -> none  [the longest x1 72.5 us: local(): lax.psum_scatter(qkv_grad, 'dp', scatter_dimension=0, tiled=True)]
    pallas_call x0 -> x1, Pallas kernels: none -> 192 us  [local(): pl.pallas_call(functools.partial(kernel, cfg), out_shape=[jax.ShapeDtypeS...]
    all_gather x6 -> x0, waiting for transfers between devices: 90.7 us -> none  [the longest x1 39 us: local(): lax.all_gather(proj_weight.astype(jnp.bfloat16), 'dp', axis=1, tiled=True)]
    all_gather x2 -> x0, blocking collectives: 69 us -> none  [the longest x1 36 us: local(): lax.all_gather(qkv_weight.astype(jnp.bfloat16), 'dp', axis=0, tiled=True)]
    psum x2 -> x0, blocking collectives: 64.7 us -> none  [the longest x1 41.3 us: local(): lax.psum((ln1_gain_grad, ln1_bias_grad, attn_out_bias_grad, ln2_gain_grad...]
    dot_general x23 -> x0, matrix products: 53.8 us -> none  [the longest x7 27.4 us: contract(): lax.dot_general(left_side, right_side, (((left_dim,), (right_dim,)), ((),...]
    all_to_all x2 -> x0, blocking collectives: 37.6 us -> none  [the longest x1 19.1 us: local(): lax.all_to_all(sent_input, 'dp', split_axis=0, concat_axis=0, tiled=True)]
    unnamed x15 -> x0, waiting for transfers between devices: 31 us -> none
  transfers between devices with their start and end apart: 16 -> 0, of which waited for: 13 -> 0; matrix products, arithmetic and copies ran while one was open for 7% -> 0% of each run, Pallas kernels for 0% -> 0%
where the time goes in v1:
time: 211 us; the launch traced here: 210 us
  Pallas kernels  192 us (91%)
  local copies, waits for them, and re-layouts  18.2 us (9%)
    pallas_call x1, Pallas kernels, local(): pl.pallas_call(functools.partial(kernel, cfg), out_shape=[jax.ShapeDtypeS...  192 us
    unnamed x35, local copies, waits for them, and re-layouts  10.7 us
    reshape x7, local copies, waits for them, and re-layouts, local(): row = lambda v: v.reshape(1, -1)  4.75 us

profile of v1, /device:TPU:0, one launch (start us, length us, event | category | flops | bytes accessed | tf_op | source)
XLA Modules:
  0.0 210.5 jit_solution(10131477423360328071)
XLA Ops:
  0.6 0.0 copy-start.6
  0.7 1.3 reshape.87.refs_4_
  1.9 0.0 copy-done.6
  1.9 0.0 copy-start.7
  1.9 0.6 reshape.88.refs_5_
  2.5 0.1 copy-done.7
  2.6 0.0 copy-start.8
  2.6 0.6 reshape.89.refs_9_
  3.2 0.1 copy-done.8
  3.3 0.0 copy-start.9
  3.3 0.6 reshape.90.refs_10_
  3.9 0.1 copy-done.9
  4.0 0.0 copy-start.10
  4.0 0.6 reshape.91.refs_11_
  4.6 0.1 copy-done.10
  4.7 0.0 copy-start.11
  4.7 0.6 reshape.92.refs_13_
  5.3 0.1 copy-done.11
  5.4 0.0 copy-start.12
  5.4 0.6 reshape.93.refs_15_
  6.0 0.1 copy-done.12
  6.1 0.7 copy.30.refs_1_
  6.7 0.0 copy-start.4
  6.7 2.0 copy.31.refs_6_
  8.7 0.0 copy-done.4
  8.7 0.9 copy.32.refs_14_
  9.6 191.6 %shard_map.263 = (bf16[8,32,768]{2,1,0:T(8,128)(2,1)}, bf16[8,32,768]{2,1,0:T(8,128)(2,1)}, f32[3,96,192]{2,1,0:T(8,128)}, f32[96,192]{1,0:T(8,128)}, f32[96,768...) custom-call(s32[8]{0:T(128)} %refs_0_.1, s32[8,4]{1,0:T(8,128)} %copy.30.refs_1_, ...), custom_call_target="tpu_custom_call" | custom-call | tf_op jit(solution)/shard_map/pallas_call | solution.py:1064
  201.2 0.0 copy-start.5
  201.2 0.7 slice.29
  201.9 0.6 reshape.98
  202.5 1.4 slice_bitcast_fusion
  203.9 0.0 copy-done.5
  203.9 0.7 copy.33
  204.7 0.0 copy-start
  204.7 1.8 copy.39
  206.5 0.0 copy-done
  206.5 0.0 copy-start.3
  206.5 0.7 copy.40
  207.3 0.4 copy-done.3
  207.6 0.0 copy-start.2
  207.6 0.7 copy.41
  208.3 0.4 copy-done.2
  208.7 0.0 copy-start.1
  208.7 0.7 copy.42
  209.4 0.4 copy-done.1
  209.7 0.7 copy.43
Async XLA Ops:
  0.6 1.3 copy-start.6
  1.9 0.7 copy-start.7
  2.6 0.7 copy-start.8
  3.3 0.7 copy-start.9
  4.0 0.7 copy-start.10
  4.7 0.7 copy-start.11
  5.4 0.7 copy-start.12
  6.7 2.0 copy-start.4
  201.2 2.7 %copy-start.5 = (f32[96,192]{1,0:T(8,128)S(1)}, f32[96,192]{1,0:T(8,128)}, u32[]{:S(2)}) copy-start(f32[96,192]{1,0:T(8,128)} %get-tuple-element.27) | copy-start | bytes 221188
  204.7 1.8 copy-start
  206.5 1.1 copy-start.3
  207.6 1.1 copy-start.2
  208.7 1.1 copy-start.1

commit v2 on v1

--- a/solution.py
+++ b/solution.py
@@ -22,6 +22,9 @@
 
 QKV, OUT, FC, PROJ = "wqkv", "wo", "w1", "w2"
 H1, GF, H2, DR = "h1", "gf", "h2", "dr"
+X_IN, G_IN = "x", "g"
+OUT_Y, OUT_X, OUT_QKV, OUT_WO = "out_y", "out_x", "out_qkv", "out_wo"
+OUT_W1, OUT_W2, OUT_EARLY, OUT_LATE = "out_w1", "out_w2", "out_early", "out_late"
 
 NN = ((1,), (0,))
 NT = ((1,), (1,))
@@ -84,6 +87,14 @@
             device_id_type=MESH,
         )
 
+    LOADS = (X_IN, G_IN, QKV, OUT, FC, PROJ)
+
+    def load(name):
+        return pltpu.make_async_copy(r[name + "_hbm"], r[name + "_in"], r.load_sem.at[LOADS.index(name)])
+
+    for name in LOADS:
+        load(name).start()
+
     barrier = pltpu.get_barrier_semaphore()
     peers = [dev((hi + k) % n, t) for k in range(1, n)] + [mate, ynb, ymate]
     for peer in peers:
@@ -121,65 +132,110 @@
         lax.fori_loop(0, n, one, 0)
         r.came[tag, rows(hi * PR, PR)] = r.sent[tag, hi]
 
+    load(X_IN).wait()
     if inside:
-        pick_pieces(0, r.x)
+        pick_pieces(0, r.x_in)
     pl.semaphore_wait(barrier, len(peers))
     if inside:
         for k in range(1, n):
             a2a_in_copy(0, k).start()
-        pick_pieces(1, r.g)
     else:
-        r.came[0] = r.x[...]
-        r.came[1] = r.g[...]
+        r.came[0] = r.x_in[...]
+    for j, vec in enumerate((r.ln1g, r.ln1b, r.aob, r.ln2g, r.ln2b, r.pjb, r.fcb)):
+        for i in range(vec.shape[0]):
+            r.vecs[j : j + 1, i * 128 : (i + 1) * 128] = vec[i : i + 1]
 
     WG = (QKV, OUT, FC, PROJ)
+    middle = (z == 1) | (z == 2)
+    side = z // 2
+    near, far_mid, far_end = z + 1 - 2 * (z % 2), 2 - side, 3 - 3 * side
+    Z_FROM = (near, far_mid, far_end)
+    near_dev = dev(2 * near + xx, t)
 
     def wslot(name, ref, slot):
         where = rows(slot * WR, WR, 16)
         return ref.at[:, where] if name == QKV else ref.at[where]
 
-    def wg_z(name, k):
+    def wg_z(name, i):
         sem = r.wg_sem
         a = WG.index(name)
-        own = wslot(name, r[name], hi)
-        return rcopy(own, own, sem.at[0, a, k], sem.at[1, a, k], zdev(k))
-
-    def wg_x(name, k):
+        if i < 2:
+            slot = wslot(name, r[name], hi)
+            target = (near_dev, dev(2 * far_mid + xx, t))[i]
+            recv = (0, jnp.where(middle, 1, 2))[i]
+        else:
+            slot = wslot(name, r[name], 2 * Z_FROM[i - 1] + xx)
+            target = near_dev
+            recv = i - 1
+        return rcopy(slot, slot, sem.at[0, a, i], sem.at[1, a, recv], target)
+
+    def wg_in(name, i):
         sem = r.wg_sem
         a = WG.index(name)
-        slot = wslot(name, r[name], 2 * ((z - k + NZ) % NZ) + xx)
-        return rcopy(slot, slot, sem.at[0, a, NZ + k], sem.at[1, a, NZ + k], xnb)
+        slot = wslot(name, r[name], 2 * Z_FROM[i] + xx)
+        return rcopy(slot, slot, sem.at[0, a, 3], sem.at[1, a, i], near_dev)
+
+    def wg_x(name, i):
+        sem = r.wg_sem
+        a = WG.index(name)
+        slot = wslot(name, r[name], 2 * (Z_FROM + (z,))[i] + xx)
+        return rcopy(slot, slot, sem.at[0, a, 4 + i], sem.at[1, a, 4 + i], xnb)
 
     def wg_start(name):
-        for k in range(1, NZ):
-            wg_z(name, k).start()
+        wg_z(name, 0).start()
+        wg_z(name, 1).start()
+
+    def wg_first(name):
+        wg_in(name, 0).wait_recv()
         wg_x(name, 0).start()
 
-    def wg_forward(name):
-        for k in range(1, NZ):
-            wg_z(name, k).wait_recv()
-            wg_x(name, k).start()
+        @pl.when(middle)
+        def _():
+            for i in (1, 2):
+                wg_in(name, i).wait_recv()
+                wg_z(name, i + 1).start()
+                wg_x(name, i).start()
+
+    def wg_second(name):
+        @pl.when(jnp.logical_not(middle))
+        def _():
+            for i in (1, 2):
+                wg_in(name, i).wait_recv()
+                wg_x(name, i).start()
 
     def wg_wait(name):
-        for k in range(NZ):
-            wg_x(name, k).wait_recv()
+        for i in range(NZ):
+            wg_x(name, i).wait_recv()
 
     def wg_drain(name):
-        for k in range(1, NZ):
-            wg_z(name, k).wait_send()
-        for k in range(NZ):
-            wg_x(name, k).wait_send()
+        for i in range(2):
+            wg_z(name, i).wait_send()
+        for i in range(NZ):
+            wg_x(name, i).wait_send()
+
+        @pl.when(middle)
+        def _():
+            for i in (2, 3):
+                wg_z(name, i).wait_send()
 
     own_w = rows(hi * WR, WR, 16)
+    for name in WG:
+        load(name).wait()
     for i in range(3):
-        r.wqkv[i, own_w] = r.qkv_in[:, i, :].astype(BF)
-    r.w1[own_w] = r.fc_in[...].astype(BF)
+        r.wqkv[i, own_w] = r.wqkv_in[i].astype(BF)
+    r.w1[own_w] = r.w1_in[...].astype(BF)
+    r.w2[own_w] = r.w2_in[...].astype(BF)
     r.turn[...] = jnp.zeros_like(r.turn)
-    r.turn[:, :WR] = r.proj_in[...].astype(F32)
-    for i in range(FH // 256):
-        r.w2[own_w, i * 256 : (i + 1) * 256] = r.turn[i * 256 : (i + 1) * 256].T[:WR].astype(BF)
-    r.turn[:HC, :WR] = r.out_in[...].astype(F32)
-    r.wo[own_w] = r.turn[:256].T[:WR, :HC].astype(BF)
+    r.turn[:HC, :WR] = r.wo_in[...].astype(F32)
+    r.wo[own_w] = r.turn[...].T[:WR, :HC].astype(BF)
+    for name in WG:
+        wg_x(name, 3).start()
+
+    load(G_IN).wait()
+    if inside:
+        pick_pieces(1, r.g_in)
+    else:
+        r.came[1] = r.g_in[...]
 
     AG = (H1, GF, H2, DR)
 
@@ -311,7 +367,7 @@
             gr_z(name, k).wait_send()
 
     tpeers = [mate, ynb, ymate]
-    SHARED = (24, 16)
+    SHARED = (32, 16)
 
     def sm_t(tag, i):
         sem = r.sm_sem
@@ -373,6 +429,7 @@
         for k in range(1, n):
             a2a_in_copy(0, k).wait_recv()
     wg_start(QKV)
+    wg_start(OUT)
 
     def norm_step(values, at, gain, bias, cen, scale):
         mean = jnp.mean(values, axis=1, keepdims=True)
@@ -400,7 +457,7 @@
             at = rows(ch * CR + s * STEP, STEP)
             values = r.came[0, at].astype(F32)
             r.h1[rows(t * B + ch * CR + s * STEP, STEP)] = norm_step(
-                values, at, r.ln1g[...], r.ln1b[...], r.cen1, r.scale1
+                values, at, r.vecs[0:1], r.vecs[1:2], r.cen1, r.scale1
             )
             return 0
 
@@ -410,9 +467,12 @@
     if inside:
         for k in range(1, n):
             a2a_in_copy(1, k).start()
-    wg_forward(QKV)
-    wg_start(OUT)
+    wg_first(QKV)
+    wg_first(OUT)
     wg_start(FC)
+    wg_start(PROJ)
+    wg_second(QKV)
+    wg_second(OUT)
     wg_wait(QKV)
 
     lane = lax.broadcasted_iota(jnp.int32, (1, HC), 1)
@@ -464,8 +524,7 @@
     lax.fori_loop(0, B // STEP, own_grad, 0)
     for ch in range(CHUNKS):
         ag_send(GF, ch)
-    wg_forward(OUT)
-    wg_start(PROJ)
+    wg_first(FC)
 
     pack = hi * (packs // n) + lo
 
@@ -473,8 +532,8 @@
         pos = i * B + lax.broadcasted_iota(jnp.int32, (1, B), 1)
         first = jnp.zeros((1, B), jnp.int32)
         end = jnp.int32(0)
-        for s in range(r.lengths.shape[1]):
-            length = r.lengths[pack, s]
+        for s in range(r.lengths.shape[0]):
+            length = r.lengths[s, pack]
             end = end + length
             first = first + jnp.where(pos >= end, length, 0)
 
@@ -537,11 +596,13 @@
         def _():
             rs_put(0, 2, part)
             rs_ship(0)
+            wg_second(FC)
 
         @pl.when(s == 2)
         def _():
             rs_put(0, 1, part)
             rs_m(0, 1).start()
+            wg_first(PROJ)
 
         @pl.when(s == 3)
         def _():
@@ -550,7 +611,6 @@
         return 0
 
     lax.fori_loop(0, 4, attend_step, 0)
-    wg_forward(FC)
 
     rs_m(0, 1).wait_recv()
     for ch in range(CHUNKS):
@@ -558,10 +618,10 @@
 
         def one(s, _):
             at = rows(ch * CR + s * STEP, STEP)
-            values = r.came[0, at].astype(F32) + rs_total(0, at) + r.aob[...]
+            values = r.came[0, at].astype(F32) + rs_total(0, at) + r.vecs[2:3]
             r.res[at] = values
             r.h2[rows(t * B + ch * CR + s * STEP, STEP)] = norm_step(
-                values, at, r.ln2g[...], r.ln2b[...], r.cen2, r.scale2
+                values, at, r.vecs[3:4], r.vecs[4:5], r.cen2, r.scale2
             )
             return 0
 
@@ -570,7 +630,7 @@
     rs_drain(0)
     ag_arrive(GF, 1)
     ag_arrive(GF, 2)
-    wg_forward(PROJ)
+    wg_second(PROJ)
     ag_arrive(GF, 3)
     wg_wait(FC)
     wg_wait(PROJ)
@@ -593,7 +653,7 @@
         grad = r.gf[at]
         for j in range(FH // 256):
             cols = slice(j * 256, (j + 1) * 256)
-            u = dot(hidden, r.w1[:, cols], NN) + r.fcb[:, cols]
+            u = dot(hidden, r.w1[:, cols], NN) + r.vecs[6:7, cols]
             dz = dot(grad, r.w2[:, cols], NN)
             square = u * u
             half = 0.5 + 0.5 * jnp.tanh(u * (CURVE + (CURVE * CUBE) * square))
@@ -647,7 +707,7 @@
 
         def one(s, _):
             at = rows(ch * CR + s * STEP, STEP)
-            back = norm_back(rs_total(1, at), at, r.ln2g[...], r.cen2, r.scale2, 2)
+            back = norm_back(rs_total(1, at), at, r.vecs[3:4], r.cen2, r.scale2, 2)
             grad = r.came[1, at].astype(F32) + back
             r.dres[at] = grad
             r.acc[4] += fold(grad)
@@ -702,6 +762,8 @@
         @pl.when(s == 3)
         def _():
             ag_arrive(DR, 3)
+            grad_tiles(r.dr, r.al, r.gwo)
+            gr_start(OUT)
 
         i = block_of(s)
         at = rows(i * B, B)
@@ -791,8 +853,6 @@
 
     lax.fori_loop(0, D // 256, grad_qkv, 0)
     gr_start(QKV)
-    grad_tiles(r.dr, r.al, r.gwo)
-    gr_start(OUT)
 
     rs_m(3, 1).wait_recv()
     for ch in range(CHUNKS):
@@ -800,7 +860,7 @@
 
     def finish_up(s, _):
         at = rows(s * STEP, STEP)
-        r.made[0, at] = (r.res[at] + rs_total(3, at) + r.pjb[...]).astype(BF)
+        r.made[0, at] = (r.res[at] + rs_total(3, at) + r.vecs[5:6]).astype(BF)
         return 0
 
     lax.fori_loop(0, B // STEP, finish_up, 0)
@@ -809,17 +869,17 @@
             a2a_out_copy(0, k).start()
         r.back0[hi] = r.made[0, rows(hi * PR, PR)]
     else:
-        r.out_y[...] = r.made[0]
+        r.out_y_v[...] = r.made[0]
 
     def line(value):
         return jnp.sum(value, axis=0, keepdims=True)
 
     for j, at in enumerate((5, 2, 3, 4)):
-        spread(0, 6 * j, line(r.acc[at]))
-    spread(0, 24, line(r.acc_f[...]))
+        spread(0, 8 * j, line(r.acc[at]))
+    spread(0, 32, line(r.acc_f[...]))
     pad = jnp.zeros((1, 256 - HC), F32)
     for j in range(2):
-        spread(0, 30 + 2 * j, jnp.concatenate([line(r.acc_h[j]), pad], axis=1))
+        spread(0, 40 + 2 * j, jnp.concatenate([line(r.acc_h[j]), pad], axis=1))
     sm_start(0)
 
     rs_m(2, 1).wait_recv()
@@ -828,7 +888,7 @@
 
         def one(s, _):
             at = rows(ch * CR + s * STEP, STEP)
-            back = norm_back(rs_total(2, at), at, r.ln1g[...], r.cen1, r.scale1, 0)
+            back = norm_back(rs_total(2, at), at, r.vecs[0:1], r.cen1, r.scale1, 0)
             r.made[1, at] = (r.dres[at] + back).astype(BF)
             return 0
 
@@ -840,17 +900,19 @@
             a2a_out_copy(1, k).start()
         r.back1[hi] = r.made[1, rows(hi * PR, PR)]
     else:
-        r.out_x[...] = r.made[1]
+        r.out_x_v[...] = r.made[1]
     for j in range(2):
-        spread(1, 6 * j, line(r.acc[j]))
+        spread(1, 8 * j, line(r.acc[j]))
     sm_start(1)
     sm_mid(0)
     gr_mid(QKV)
     gr_mid(OUT)
     sm_mid(1)
 
-    r.out_w2[...] = gr_finish(PROJ)
-    r.out_w1[...] = gr_finish(FC)
+    OUTS = tuple(outputs(cfg))
+
+    def store(name):
+        return pltpu.make_async_copy(r[name + "_v"], r[name], r.store_sem.at[OUTS.index(name)])
 
     def put_back(tag, out):
         for k in range(1, n):
@@ -862,20 +924,34 @@
 
         lax.fori_loop(0, n, one, 0)
 
+    r.out_w2_v[...] = gr_finish(PROJ)
+    store(OUT_W2).start()
+    r.out_w1_v[...] = gr_finish(FC)
+    store(OUT_W1).start()
     if inside:
-        put_back(0, r.out_y)
-    r.out_early[...] = sm_finish(0)
-    r.out_qkv[...] = gr_finish(QKV)
-    r.out_wo[...] = gr_finish(OUT)
-    r.out_late[...] = sm_finish(1)
+        put_back(0, r.out_y_v)
+    store(OUT_Y).start()
+    r.turn[...] = jnp.zeros_like(r.turn)
+    r.turn[:WR, :HC] = gr_finish(OUT)
+    r.out_wo_v[...] = r.turn[...].T[:HC, :WR]
+    store(OUT_WO).start()
+    r.out_early_v[...] = sm_finish(0)
+    store(OUT_EARLY).start()
     if inside:
-        put_back(1, r.out_x)
+        put_back(1, r.out_x_v)
+    store(OUT_X).start()
+    r.out_late_v[...] = sm_finish(1)
+    store(OUT_LATE).start()
+    r.out_qkv_v[...] = gr_finish(QKV)
+    store(OUT_QKV).start()
 
     for name in WG:
         wg_drain(name)
         gr_drain(name)
     for name in AG:
         ag_drain(name)
+    for name in OUTS:
+        store(name).wait()
     for tag in range(2):
         sm_drain(tag)
         if inside:
@@ -884,25 +960,42 @@
                 a2a_out_copy(tag, k).wait_send()
 
 
+def settle(*refs):
+    early, late = refs[6:8]
+    whole, small = refs[8:14], refs[14:22]
+    for i in range(6):
+        whole[i][...] = refs[i][...]
+    for j in range(4):
+        small[j][...] = early[8 * j : 8 * j + small[j].shape[0]]
+    for j in range(2):
+        small[4 + j][...] = late[8 * j : 8 * j + small[4 + j].shape[0]]
+    small[6][...] = early[32 : 32 + small[6].shape[0]]
+    heads = small[7]
+    for j in range(2):
+        heads[j : j + 1, :128] = early[40 + 2 * j : 41 + 2 * j]
+        heads[j : j + 1, 128:] = early[41 + 2 * j : 42 + 2 * j, : heads.shape[1] - 128]
+
+
 def inputs():
     vmem = pl.BlockSpec(memory_space=pltpu.VMEM)
     smem = pl.BlockSpec(memory_space=pltpu.SMEM)
+    hbm = pl.BlockSpec(memory_space=pl.ANY)
     return Refs(
         order=smem,
         lengths=smem,
-        x=vmem,
-        g=vmem,
+        x_hbm=hbm,
+        g_hbm=hbm,
         ln1g=vmem,
         ln1b=vmem,
-        qkv_in=vmem,
+        wqkv_hbm=hbm,
         qvb=vmem,
-        out_in=vmem,
+        wo_hbm=hbm,
         aob=vmem,
         ln2g=vmem,
         ln2b=vmem,
-        fc_in=vmem,
+        w1_hbm=hbm,
         fcb=vmem,
-        proj_in=vmem,
+        w2_hbm=hbm,
         pjb=vmem,
     )
 
@@ -915,10 +1008,10 @@
         out_y=(tokens, BF),
         out_x=(tokens, BF),
         out_qkv=((3, WR, HC), F32),
-        out_wo=((WR, HC), F32),
+        out_wo=((HC, WR), F32),
         out_w1=((WR, FH), F32),
         out_w2=((WR, FH), F32),
-        out_early=((40, 128), F32),
+        out_early=((48, 128), F32),
         out_late=((16, 128), F32),
     )
 
@@ -931,6 +1024,8 @@
     V = pltpu.VMEM
     sem = pltpu.SemaphoreType.DMA
     blocks = S // L
+    tokens = (n, L // n, D) if inside else (L, D)
+    kind = F32 if inside else BF
     made = Refs(
         came=V((2, L, D), BF),
         made=V((2, L, D), BF),
@@ -938,7 +1033,16 @@
         wo=V((D, HC), BF),
         w1=V((D, FH), BF),
         w2=V((D, FH), BF),
-        turn=V((FH, 128), F32),
+        turn=V((256, 256), F32),
+        vecs=V((8, D), F32),
+        x_in=V(tokens, BF),
+        g_in=V(tokens, BF),
+        wqkv_in=V((3, WR, HC), kind),
+        wo_in=V((HC, WR), kind),
+        w1_in=V((WR, FH), kind),
+        w2_in=V((WR, FH), kind),
+        load_sem=sem((6,)),
+        store_sem=sem((8,)),
         h1=V((S, D), BF),
         gf=V((S, D), BF),
         h2=V((S, D), BF),
@@ -970,11 +1074,13 @@
         acc=V((6, 8, D), F32),
         acc_f=V((8, FH), F32),
         acc_h=V((2, 8, HC), F32),
-        slab0=V((4, 40, 128), F32),
+        slab0=V((4, 48, 128), F32),
         slab1=V((4, 16, 128), F32),
-        hslab0=V((n, 40, 128), F32),
+        hslab0=V((n, 48, 128), F32),
         hslab1=V((n, 16, 128), F32),
     )
+    for name, (shape, dtype) in outputs(cfg).items():
+        made[name + "_v"] = V(shape, dtype)
     if inside:
         made.update(
             sent=V((2, n, L // n, D), BF),
@@ -1059,24 +1165,24 @@
             lax.all_gather(w.astype(BF), "lo", axis=axis, tiled=True)
             for w, axis in zip(weights, (0, 1, 0, 1))
         ]
-    row = lambda v: v.reshape(1, -1)
+    row = lambda v: v.reshape(-1, 128)
     outs = outputs(cfg)
     made = pl.pallas_call(
         functools.partial(kernel, cfg),
         out_shape=[jax.ShapeDtypeStruct(shape, kind) for shape, kind in outs.values()],
         in_specs=list(inputs().values()),
-        out_specs=[pl.BlockSpec(memory_space=pltpu.VMEM)] * len(outs),
+        out_specs=[pl.BlockSpec(memory_space=pl.ANY)] * len(outs),
         scratch_shapes=list(scratch(cfg).values()),
         compiler_params=pltpu.CompilerParams(
             collective_id=0, has_side_effects=True, vmem_limit_bytes=63 * 2**20
         ),
     )(
         pack_order,
-        seq_lengths,
+        seq_lengths.T,
         *tokens,
         row(ln1_gain),
         row(ln1_bias),
-        weights[0],
+        jnp.transpose(weights[0], (1, 0, 2)),
         qv_bias,
         weights[1],
         row(attn_out_bias),
@@ -1084,51 +1190,48 @@
         row(ln2_bias),
         weights[2],
         row(fc_bias),
-        weights[3],
+        weights[3].T,
         row(proj_bias),
     )
     g = Refs(zip(outs, made))
-    out_y, out_x = g.out_y, g.out_x
-    qkv_sum = jnp.transpose(g.out_qkv, (1, 0, 2))
-    out_sum = g.out_wo.T
-    fc_sum = g.out_w1
-    proj_sum = g.out_w2.T
-    early, late = g.out_early, g.out_late
-    if inside:
-        out_y, out_x = out_y.reshape(L, D), out_x.reshape(L, D)
-    else:
-        out_y, out_x = [
-            pick(
-                chosen.T,
-                lax.all_to_all(v, ("hi", "lo"), split_axis=0, concat_axis=0, tiled=True),
-            )
-            for v in (out_y, out_x)
-        ]
-        qkv_sum, out_sum, fc_sum, proj_sum = [
-            lax.psum_scatter(w, "lo", scatter_dimension=axis, tiled=True)
-            for w, axis in ((qkv_sum, 0), (out_sum, 1), (fc_sum, 0), (proj_sum, 1))
-        ]
-        early, late = lax.psum((early, late), "lo")
+    if not inside:
+        exchange = lambda v: pick(
+            chosen.T,
+            lax.all_to_all(v, ("hi", "lo"), split_axis=0, concat_axis=0, tiled=True),
+        )
+        share = lambda v, axis: lax.psum_scatter(v, "lo", scatter_dimension=axis, tiled=True)
+        g.out_y, g.out_x = exchange(g.out_y), exchange(g.out_x)
+        g.out_qkv, g.out_wo = share(g.out_qkv, 1), share(g.out_wo, 1)
+        g.out_w1, g.out_w2 = share(g.out_w1, 0), share(g.out_w2, 0)
+        g.out_early, g.out_late = lax.psum((g.out_early, g.out_late), "lo")
+    whole = [g.out_y.reshape(L, D), g.out_x.reshape(L, D), g.out_qkv, g.out_wo, g.out_w1, g.out_w2]
     vec = D // 128
-    shared = [early[j * vec : (j + 1) * vec].reshape(D) for j in range(4)]
-    fc_bias_sum = early[4 * vec : 4 * vec + FH // 128].reshape(FH)
-    head = 4 * vec + FH // 128
-    qv_sum = early[head : head + 4].reshape(2, 256)[:, :HC]
+    vmem = pl.BlockSpec(memory_space=pltpu.VMEM)
+    settled = pl.pallas_call(
+        settle,
+        out_shape=[jax.ShapeDtypeStruct(v.shape, v.dtype) for v in whole]
+        + [jax.ShapeDtypeStruct((vec, 128), F32)] * 6
+        + [jax.ShapeDtypeStruct((FH // 128, 128), F32), jax.ShapeDtypeStruct((2, HC), F32)],
+        in_specs=[vmem] * 8,
+        out_specs=[vmem] * 14,
+    )(*whole, g.out_early, g.out_late)
+    out_y, out_x, qkv_sum, out_sum, fc_sum, proj_sum = settled[:6]
+    pjb, ln2g, ln2b, aob, ln1g, ln1b = [v.reshape(D) for v in settled[6:12]]
     return (
         out_y,
         out_x,
-        late[:vec].reshape(D),
-        late[vec : 2 * vec].reshape(D),
-        qkv_sum,
-        qv_sum,
+        ln1g,
+        ln1b,
+        jnp.transpose(qkv_sum, (1, 0, 2)),
+        settled[13],
         out_sum,
-        shared[3],
-        shared[1],
-        shared[2],
+        aob,
+        ln2g,
+        ln2b,
         fc_sum,
-        fc_bias_sum,
-        proj_sum,
-        shared[0],
+        settled[12].reshape(FH),
+        proj_sum.T,
+        pjb,
     )
 
 

time: 211 us -> 175 us (0.83)
  local copies, waits for them, and re-layouts: 18.2 us -> 0 us
  Pallas kernels: 192 us -> 174 us
    pallas_call x1, Pallas kernels: 192 us -> 172 us  [local(): pl.pallas_call(functools.partial(kernel, cfg), out_shape=[jax.ShapeDtypeS...]
    unnamed x35 -> x0, local copies, waits for them, and re-layouts: 10.7 us -> none
    reshape x9 -> x0, local copies, waits for them, and re-layouts: 6.74 us -> none  [the longest x7 4.75 us: local(): row = lambda v: v.reshape(1, -1)]
    pallas_call x0 -> x1, Pallas kernels: none -> 2.71 us  [local(): pl.pallas_call(settle, out_shape=[jax.ShapeDtypeStruct(v.shape, v.dtype)...]
where the time goes in v2:
time: 175 us
  Pallas kernels  174 us (99%)
    pallas_call x1, Pallas kernels, local(): pl.pallas_call(functools.partial(kernel, cfg), out_shape=[jax.ShapeDtypeS...  172 us

profile of v2, /device:TPU:0, one launch (start us, length us, event | category | flops | bytes accessed | tf_op | source)
XLA Modules:
  0.0 175.0 jit_solution(13001650448893725732)
XLA Ops:
  0.7 171.6 %shard_map.263 = (bf16[8,32,768]{2,1,0:T(8,128)(2,1)}, bf16[8,32,768]{2,1,0:T(8,128)(2,1)}, f32[3,96,192]{2,1,0:T(8,128)}, f32[192,96]{1,0:T(8,128)}, f32[96,768...) custom-call(s32[8]{0:T(128)} %refs_0_.1, s32[4,8]{1,0:T(4,128)} %bitcast.36, ...), custom_call_target="tpu_custom_call" | custom-call | tf_op jit(solution)/shard_map/pallas_call | solution.py:1170
  172.3 2.7 %shard_map.264 = (bf16[256,768]{1,0:T(8,128)(2,1)}, bf16[256,768]{1,0:T(8,128)(2,1)}, f32[3,96,192]{2,1,0:T(8,128)}, f32[192,96]{1,0:T(8,128)}, f32[96,768]{1,0:...) custom-call(bf16[256,768]{1,0:T(8,128)(2,1)} %bitcast.23, ...), custom_call_target="tpu_custom_call" | custom-call | tf_op jit(solution)/shard_map/pallas_call | solution.py:1210

commit v3 on v2

--- a/solution.py
+++ b/solution.py
@@ -20,7 +20,8 @@
 CHUNKS = 2
 STEP = 32
 
-QKV, OUT, FC, PROJ = "wqkv", "wo", "w1", "w2"
+PAIR, LAST, OUT, FC, PROJ = "wa", "wb", "wo", "w1", "w2"
+QKV = "wqkv"
 H1, GF, H2, DR = "h1", "gf", "h2", "dr"
 X_IN, G_IN = "x", "g"
 OUT_Y, OUT_X, OUT_QKV, OUT_WO = "out_y", "out_x", "out_qkv", "out_wo"
@@ -48,11 +49,15 @@
     slabs, hslabs = (r.slab0, r.slab1), (r.hslab0, r.hslab1)
     backs = (r.back0, r.back1) if inside else None
     NH = HC // HEAD_DIM
+    LW = HEAD_DIM
+    PW = HC - LW
     NZ = n // 2
     WR = D // n
     PR = L // n
     CR = L // CHUNKS
     B = L
+    KS = 2
+    KB = KS * B
 
     hi = lax.axis_index("hi")
     lo = lax.axis_index("lo")
@@ -145,7 +150,8 @@
         for i in range(vec.shape[0]):
             r.vecs[j : j + 1, i * 128 : (i + 1) * 128] = vec[i : i + 1]
 
-    WG = (QKV, OUT, FC, PROJ)
+    WG = (PAIR, LAST, OUT, FC, PROJ)
+    STRAIGHT = (PAIR, LAST, OUT)
     middle = (z == 1) | (z == 2)
     side = z // 2
     near, far_mid, far_end = z + 1 - 2 * (z % 2), 2 - side, 3 - 3 * side
@@ -153,8 +159,7 @@
     near_dev = dev(2 * near + xx, t)
 
     def wslot(name, ref, slot):
-        where = rows(slot * WR, WR, 16)
-        return ref.at[:, where] if name == QKV else ref.at[where]
+        return ref.at[rows(slot * WR, WR, 16)]
 
     def wg_z(name, i):
         sem = r.wg_sem
@@ -163,6 +168,10 @@
             slot = wslot(name, r[name], hi)
             target = (near_dev, dev(2 * far_mid + xx, t))[i]
             recv = (0, jnp.where(middle, 1, 2))[i]
+        elif name in STRAIGHT:
+            slot = wslot(name, r[name], hi)
+            target = dev(2 * far_end + xx, t)
+            recv = jnp.where(middle, 1, 2)
         else:
             slot = wslot(name, r[name], 2 * Z_FROM[i - 1] + xx)
             target = near_dev
@@ -188,6 +197,8 @@
     def wg_first(name):
         wg_in(name, 0).wait_recv()
         wg_x(name, 0).start()
+        if name in STRAIGHT:
+            return
 
         @pl.when(middle)
         def _():
@@ -197,6 +208,12 @@
                 wg_x(name, i).start()
 
     def wg_second(name):
+        if name in STRAIGHT:
+            for i in (1, 2):
+                wg_in(name, i).wait_recv()
+                wg_x(name, i).start()
+            return
+
         @pl.when(jnp.logical_not(middle))
         def _():
             for i in (1, 2):
@@ -212,6 +229,9 @@
             wg_z(name, i).wait_send()
         for i in range(NZ):
             wg_x(name, i).wait_send()
+        if name in STRAIGHT:
+            wg_z(name, 2).wait_send()
+            return
 
         @pl.when(middle)
         def _():
@@ -219,18 +239,24 @@
                 wg_z(name, i).wait_send()
 
     own_w = rows(hi * WR, WR, 16)
-    for name in WG:
+    load(QKV).wait()
+    for i in range(3):
+        part = r.wqkv_in[i].astype(BF)
+        r.wa[own_w, i * PW : (i + 1) * PW] = part[:, :PW]
+        r.wb[own_w, i * LW : (i + 1) * LW] = part[:, PW:]
+    for name in (PAIR, LAST):
+        wg_x(name, 3).start()
+        wg_z(name, 0).start()
+    for name in LOADS[3:]:
         load(name).wait()
-    for i in range(3):
-        r.wqkv[i, own_w] = r.wqkv_in[i].astype(BF)
     r.w1[own_w] = r.w1_in[...].astype(BF)
     r.w2[own_w] = r.w2_in[...].astype(BF)
     r.turn[...] = jnp.zeros_like(r.turn)
     r.turn[:HC, :WR] = r.wo_in[...].astype(F32)
     r.wo[own_w] = r.turn[...].T[:WR, :HC].astype(BF)
-    for name in WG:
+    for name in (OUT, FC, PROJ):
         wg_x(name, 3).start()
-
+    wg_z(OUT, 0).start()
     load(G_IN).wait()
     if inside:
         pick_pieces(1, r.g_in)
@@ -329,42 +355,89 @@
         slot = wslot(name, r[GR[name]], 2 * k + 1 - xx)
         return rcopy(slot, r[name + "_xr"].at[k], sem.at[0, a, k], sem.at[1, a, k], xnb)
 
-    def gr_z(name, k):
+    def gr_z(name, i):
         sem = r.gr_sem
         a = WG.index(name)
-        return rcopy(
-            r[name + "_zs"].at[k - 1],
-            r[name + "_zr"].at[k - 1],
-            sem.at[0, a, NZ + k],
-            sem.at[1, a, NZ + k],
-            zdev(k),
-        )
+        to_mid, to_end = dev(2 * far_mid + xx, t), dev(2 * far_end + xx, t)
+        if name == PROJ:
+            to, source = (near_dev, to_mid, to_end)[i], i
+            recv = 0 if i == 0 else jnp.where(middle, 1, 2)
+        else:
+            to = {0: near_dev, 2: near_dev, 3: near_dev, 1: to_mid, 4: to_end}[i]
+            source = {0: 0, 2: 1, 3: 2, 1: 1, 4: 2}[i]
+            recv = 1 if i == 4 else i
+        part = r[name + "_zs"].at[source]
+        return rcopy(part, r[name + "_zr"].at[recv], sem.at[0, a, NZ + i], sem.at[1, a, NZ + recv], to)
+
+    def gr_zin(name, i):
+        sem = r.gr_sem
+        a = WG.index(name)
+        part = r[name + "_zr"].at[i]
+        return rcopy(part, part, sem.at[0, a, NZ], sem.at[1, a, NZ + i], near_dev)
 
     def gr_start(name):
         for k in range(NZ):
             gr_x(name, k).start()
 
+    def gr_pair(name, to):
+        mine = wslot(name, r[GR[name]], 2 * to + xx)[...].astype(F32)
+        return mine + r[name + "_xr"][to].astype(F32)
+
     def gr_mid(name):
         for k in range(NZ):
             gr_x(name, k).wait_recv()
-        for k in range(1, NZ):
-            to = (z + k) % NZ
-            mine = wslot(name, r[GR[name]], 2 * to + xx)[...].astype(F32)
-            r[name + "_zs"][k - 1] = (mine + r[name + "_xr"][to].astype(F32)).astype(BF)
-            gr_z(name, k).start()
+        zs = r[name + "_zs"]
+        zs[0] = gr_pair(name, near).astype(BF)
+        gr_z(name, 0).start()
+        if name == PROJ:
+            for i in (1, 2):
+                zs[i] = gr_pair(name, Z_FROM[i]).astype(BF)
+                gr_z(name, i).start()
+            return
+
+        @pl.when(jnp.logical_not(middle))
+        def _():
+            zs[1] = gr_pair(name, far_mid).astype(BF)
+            gr_z(name, 2).start()
+            zs[2] = gr_pair(name, far_end).astype(BF)
+            gr_z(name, 3).start()
+
+    def gr_far(name):
+        @pl.when(middle)
+        def _():
+            zs, zr = r[name + "_zs"], r[name + "_zr"]
+            gr_zin(name, 2).wait_recv()
+            zs[1] = (gr_pair(name, far_mid) + zr[2].astype(F32)).astype(BF)
+            gr_z(name, 1).start()
+            gr_zin(name, 3).wait_recv()
+            zs[2] = (gr_pair(name, far_end) + zr[3].astype(F32)).astype(BF)
+            gr_z(name, 4).start()
 
     def gr_finish(name):
-        total = wslot(name, r[GR[name]], hi)[...].astype(F32) + r[name + "_xr"][z].astype(F32)
-        for k in range(1, NZ):
-            gr_z(name, k).wait_recv()
-            total = total + r[name + "_zr"][k - 1].astype(F32)
+        total = gr_pair(name, z)
+        for i in range(3 if name == PROJ else 2):
+            gr_zin(name, i).wait_recv()
+            total = total + r[name + "_zr"][i].astype(F32)
         return total
 
     def gr_drain(name):
         for k in range(NZ):
             gr_x(name, k).wait_send()
-        for k in range(1, NZ):
-            gr_z(name, k).wait_send()
+        gr_z(name, 0).wait_send()
+        if name == PROJ:
+            gr_z(name, 1).wait_send()
+            gr_z(name, 2).wait_send()
+            return
+
+        @pl.when(middle)
+        def _():
+            gr_z(name, 1).wait_send()
+            gr_z(name, 4).wait_send()
+
+        @pl.when(jnp.logical_not(middle))
+        def _():
+            gr_z(name, 2).wait_send()
+            gr_z(name, 3).wait_send()
 
     tpeers = [mate, ynb, ymate]
     SHARED = (32, 16)
@@ -423,13 +496,15 @@
         slab[t] = jnp.zeros(slab.shape[1:], F32)
     r.acc[...] = jnp.zeros_like(r.acc)
     r.acc_f[...] = jnp.zeros_like(r.acc_f)
-    r.acc_h[...] = jnp.zeros_like(r.acc_h)
+    r.acc_a[...] = jnp.zeros_like(r.acc_a)
+    r.acc_b[...] = jnp.zeros_like(r.acc_b)
 
     if inside:
         for k in range(1, n):
             a2a_in_copy(0, k).wait_recv()
-    wg_start(QKV)
-    wg_start(OUT)
+    for name in STRAIGHT:
+        wg_z(name, 1).start()
+        wg_z(name, 2).start()
 
     def norm_step(values, at, gain, bias, cen, scale):
         mean = jnp.mean(values, axis=1, keepdims=True)
@@ -464,31 +539,26 @@
         lax.fori_loop(0, CR // STEP, one, 0)
         ag_send(H1, ch)
 
+    for name in STRAIGHT:
+        wg_first(name)
+    wg_second(PAIR)
+    ag_arrive(H1, 1)
+    ag_arrive(H1, 2)
+    wg_second(LAST)
+    wg_second(OUT)
     if inside:
         for k in range(1, n):
             a2a_in_copy(1, k).start()
-    wg_first(QKV)
-    wg_first(OUT)
     wg_start(FC)
-    wg_start(PROJ)
-    wg_second(QKV)
-    wg_second(OUT)
-    wg_wait(QKV)
-
-    lane = lax.broadcasted_iota(jnp.int32, (1, HC), 1)
+    wg_wait(PAIR)
+    wg_wait(LAST)
+
+    lane = lax.broadcasted_iota(jnp.int32, (1, PW), 1)
 
     def head_mask(h):
         return (lane >= h * HEAD_DIM) & (lane < (h + 1) * HEAD_DIM)
 
     def project(s, _):
-        @pl.when(s == 1)
-        def _():
-            ag_arrive(H1, 1)
-
-        @pl.when(s == 2)
-        def _():
-            ag_arrive(H1, 2)
-
         @pl.when(s == 3)
         def _():
             ag_arrive(H1, 3)
@@ -496,23 +566,33 @@
         b = block_of(s)
         at = rows(b * B, B)
         hidden = r.h1[at]
-        q = dot(hidden, r.wqkv[0], NN) + r.qvb[0:1]
-        q = (q.astype(BF).astype(F32) * HEAD_DIM ** (-0.5)).astype(BF)
-        for h in range(NH):
-            r.qm[b, h * B : (h + 1) * B] = jnp.where(head_mask(h), q, jnp.zeros_like(q))
-        k = dot(hidden, r.wqkv[1], NN)
-        r.k[at] = k.astype(BF)
-        r.kt[:, at] = k.T.astype(BF)
-        v = dot(hidden, r.wqkv[2], NN) + r.qvb[1:2]
-        r.v[at] = v.astype(BF)
-        r.vt[:, at] = v.T.astype(BF)
+
+        def scaled(q):
+            return (q.astype(BF).astype(F32) * HEAD_DIM ** (-0.5)).astype(BF)
+
+        both = dot(hidden, r.wa[...], NN)
+        q = scaled(both[:, :PW] + r.qvb[0:1, :PW])
+        for h in range(NH - 1):
+            r.qa[b, h * B : (h + 1) * B] = jnp.where(head_mask(h), q, jnp.zeros_like(q))
+        k = both[:, PW : 2 * PW]
+        r.ka[at] = k.astype(BF)
+        r.kt[:PW, at] = k.T.astype(BF)
+        v = both[:, 2 * PW :] + r.qvb[1:2, :PW]
+        r.va[at] = v.astype(BF)
+        r.vt[:PW, at] = v.T.astype(BF)
+        last = dot(hidden, r.wb[...], NN)
+        r.qb[b] = scaled(last[:, :LW] + r.qvb[0:1, PW:])
+        r.kb[at] = last[:, LW : 2 * LW].astype(BF)
+        r.vb[at] = (last[:, 2 * LW :] + r.qvb[1:2, PW:]).astype(BF)
+        turned = last.T
+        r.kt[PW:, at] = turned[LW : 2 * LW].astype(BF)
+        r.vt[PW:, at] = (turned[2 * LW :] + r.vbt[...]).astype(BF)
         return 0
 
+    bias_last = jnp.concatenate([r.qvb[1:2, PW:], jnp.zeros((1, LW), F32)], axis=1)
+    r.vbt[...] = jnp.broadcast_to(bias_last, (8, 2 * LW)).T[:LW, :1]
     lax.fori_loop(0, 4, project, 0)
-
-    if inside:
-        for k in range(1, n):
-            a2a_in_copy(1, k).wait_recv()
+    wg_start(PROJ)
 
     def own_grad(s, _):
         at = rows(s * STEP, STEP)
@@ -521,10 +601,14 @@
         r.acc[5] += fold(value.astype(F32))
         return 0
 
-    lax.fori_loop(0, B // STEP, own_grad, 0)
-    for ch in range(CHUNKS):
-        ag_send(GF, ch)
-    wg_first(FC)
+    def grad_in():
+        if inside:
+            for k in range(1, n):
+                a2a_in_copy(1, k).wait_recv()
+        lax.fori_loop(0, B // STEP, own_grad, 0)
+        for ch in range(CHUNKS):
+            ag_send(GF, ch)
+
 
     pack = hi * (packs // n) + lo
 
@@ -538,33 +622,37 @@
             first = first + jnp.where(pos >= end, length, 0)
 
         def scores(j, peak):
-            key_pos = j * B + lax.broadcasted_iota(jnp.int32, (B, B), 0)
+            key_pos = j * KB + lax.broadcasted_iota(jnp.int32, (KB, B), 0)
             allowed = (key_pos >= first) & (key_pos <= pos)
-            keys = r.k[rows(j * B, B)]
+            kr = rows(j * KB, KB)
+            keys, keys_last = r.ka[kr], r.kb[kr]
             peaks = []
             for h in range(NH):
-                raw = dot(keys, r.qm[i, h * B : (h + 1) * B], NT)
+                if h < NH - 1:
+                    raw = dot(keys, r.qa[i, h * B : (h + 1) * B], NT)
+                else:
+                    raw = dot(keys_last, r.qb[i], NT)
                 raw = jnp.where(allowed, raw, MASKED)
-                r.score[j, :, h * B : (h + 1) * B] = raw
+                r.score[kr, h * B : (h + 1) * B] = raw
                 peaks.append(jnp.max(raw, axis=0, keepdims=True))
             return jnp.maximum(peak, jnp.concatenate(peaks, axis=1))
 
-        peak = lax.fori_loop(0, i + 1, scores, jnp.full((1, NH * B), MASKED, F32))
+        peak = lax.fori_loop(0, (i + KS) // KS, scores, jnp.full((1, NH * B), MASKED, F32))
         r.att[...] = jnp.zeros_like(r.att)
 
         def weigh(j, total):
             totals = []
             for h in range(NH):
                 cols = slice(h * B, (h + 1) * B)
-                weight = jnp.exp(r.score[j, :, cols] - peak[:, cols])
+                weight = jnp.exp(r.score[rows(j * KB, KB), cols] - peak[:, cols])
                 totals.append(jnp.sum(weight, axis=0, keepdims=True))
                 low = weight.astype(BF)
-                r.e[i, j, :, cols] = low
+                r.e[i, rows(j * KB, KB), cols] = low
                 part = slice(h * HEAD_DIM, (h + 1) * HEAD_DIM)
-                r.att[part] += dot(r.vt[part, rows(j * B, B)], low, NN)
+                r.att[part] += dot(r.vt[part, rows(j * KB, KB)], low, NN)
             return total + jnp.concatenate(totals, axis=1)
 
-        total = lax.fori_loop(0, i + 1, weigh, jnp.zeros((1, NH * B), F32))
+        total = lax.fori_loop(0, (i + KS) // KS, weigh, jnp.zeros((1, NH * B), F32))
         inverse = 1.0 / total
         for h in range(NH):
             part = slice(h * HEAD_DIM, (h + 1) * HEAD_DIM)
@@ -591,18 +679,18 @@
         def _():
             rs_put(0, 3, part)
             rs_m(0, 0).start()
+            grad_in()
 
         @pl.when(s == 1)
         def _():
             rs_put(0, 2, part)
             rs_ship(0)
-            wg_second(FC)
 
         @pl.when(s == 2)
         def _():
             rs_put(0, 1, part)
             rs_m(0, 1).start()
-            wg_first(PROJ)
+            wg_first(FC)
 
         @pl.when(s == 3)
         def _():
@@ -611,6 +699,10 @@
         return 0
 
     lax.fori_loop(0, 4, attend_step, 0)
+    wg_second(FC)
+    ag_arrive(GF, 1)
+    ag_arrive(GF, 2)
+    wg_first(PROJ)
 
     rs_m(0, 1).wait_recv()
     for ch in range(CHUNKS):
@@ -628,8 +720,6 @@
         lax.fori_loop(0, CR // STEP, one, 0)
         ag_send(H2, ch)
     rs_drain(0)
-    ag_arrive(GF, 1)
-    ag_arrive(GF, 2)
     wg_second(PROJ)
     ag_arrive(GF, 3)
     wg_wait(FC)
@@ -699,7 +789,6 @@
     grad_tiles(r.gf, r.zz, r.gw2)
     gr_start(PROJ)
     grad_tiles(r.h2, r.du, r.gw1)
-    gr_start(FC)
 
     rs_m(1, 1).wait_recv()
     for ch in range(CHUNKS):
@@ -743,13 +832,82 @@
         return 0
 
     lax.fori_loop(0, 4, upper, 0)
-    gr_mid(PROJ)
-    gr_mid(FC)
-
-    r.dk[...] = jnp.zeros_like(r.dk)
-    r.dv[...] = jnp.zeros_like(r.dv)
-
-    def attend_back(s, _):
+    gr_start(FC)
+
+    PASS = (
+        (0, PW, NH - 1, r.qa, r.ka, r.va, r.dama, r.dka, r.dva, r.dqa),
+        (PW, LW, 1, r.qb, r.kb, r.vb, r.damb, r.dkb, r.dvb, r.dqb),
+    )
+
+    def attend_back(which, s):
+        first, width, heads, q, k, v, dam, dk, dv, dqkv = PASS[which]
+        cols = slice(first, first + width)
+        i = block_of(s)
+        at = rows(i * B, B)
+        da = dot(r.dr[at], r.wo[:, cols], NN).astype(BF).astype(F32)
+        by_row = r.inv[i].T
+        if which == 0:
+            scale = by_row[:, heads - 1 : heads]
+            for h in range(heads - 1):
+                scale = jnp.where(head_mask(h), by_row[:, h : h + 1], scale)
+        else:
+            scale = by_row[:, NH - 1 : NH]
+        low = (da * scale).astype(BF)
+        for h in range(heads):
+            dam[h * B : (h + 1) * B] = (
+                jnp.where(head_mask(h), low, jnp.zeros_like(low)) if which == 0 else low
+            )
+        if which == 0:
+            lined = (low.astype(F32) * r.a[at, :PW]).T
+        else:
+            both = low.astype(F32) * r.a[at, PW:]
+            lined = jnp.concatenate([both, both], axis=1).T
+        deltas = [
+            jnp.sum(lined[h * HEAD_DIM : (h + 1) * HEAD_DIM], axis=0, keepdims=True)
+            for h in range(heads)
+        ]
+        r.att[cols] = jnp.zeros((width, B), F32)
+
+        def over_keys(j, _):
+            kr = rows(j * KB, KB)
+            values = v[kr]
+            base = first // HEAD_DIM * B
+            for h in range(heads):
+                own = slice(h * B, (h + 1) * B)
+                dp = dot(values, dam[own], NT)
+                weight = r.e[i, kr, base + h * B : base + (h + 1) * B]
+                ds = (weight.astype(F32) * (dp - deltas[h])).astype(BF)
+                r.ds[:, own] = ds
+                part = slice(first + h * HEAD_DIM, first + (h + 1) * HEAD_DIM)
+                r.att[part] += dot(r.kt[part, kr], ds, NN)
+            dk[kr] += dot(r.ds[:, : heads * B], q[i], NN)
+            dv[kr] += dot(r.e[i, kr, base : base + heads * B], dam[...], NN)
+            return 0
+
+        lax.fori_loop(0, (i + KS) // KS, over_keys, 0)
+        if which == 0:
+            dq = r.att[cols].T
+        else:
+            dq = jnp.concatenate([r.att[cols], r.att[cols]], axis=0).T[:, :width]
+        dqkv[at, :width] = (dq * HEAD_DIM ** (-0.5)).astype(BF)
+
+    def round_kv(which):
+        first, width, _, _, _, _, _, dk, dv, dqkv = PASS[which]
+
+        def one(b, _):
+            at = rows(b * B, B)
+            dqkv[at, width : 2 * width] = dk[at].astype(BF)
+            dqkv[at, 2 * width :] = dv[at].astype(BF)
+            acc = (r.acc_a, r.acc_b)[which]
+            acc[...] += fold(dqkv[at].astype(F32))
+            return 0
+
+        lax.fori_loop(0, 4, one, 0)
+
+    for zeroed in (r.dka, r.dva, r.dkb, r.dvb):
+        zeroed[...] = jnp.zeros_like(zeroed)
+
+    def pair_step(s, _):
         @pl.when(s == 1)
         def _():
             ag_arrive(DR, 1)
@@ -758,6 +916,7 @@
         def _():
             ag_arrive(DR, 2)
             rs_ship(3)
+            gr_mid(PROJ)
 
         @pl.when(s == 3)
         def _():
@@ -765,61 +924,53 @@
             grad_tiles(r.dr, r.al, r.gwo)
             gr_start(OUT)
 
-        i = block_of(s)
-        at = rows(i * B, B)
-        da = dot(r.dr[at], r.wo[...], NN).astype(BF).astype(F32)
-        by_row = r.inv[i].T
-        scale = by_row[:, NH - 1 : NH]
-        for h in range(NH - 1):
-            scale = jnp.where(head_mask(h), by_row[:, h : h + 1], scale)
-        low = (da * scale).astype(BF)
-        for h in range(NH):
-            r.dam[h * B : (h + 1) * B] = jnp.where(head_mask(h), low, jnp.zeros_like(low))
-        lined = (low.astype(F32) * r.a[at]).T
-        deltas = [
-            jnp.sum(lined[h * HEAD_DIM : (h + 1) * HEAD_DIM], axis=0, keepdims=True)
-            for h in range(NH)
-        ]
-        r.att[...] = jnp.zeros_like(r.att)
-
-        def over_keys(j, _):
-            kr = rows(j * B, B)
-            values = r.v[kr]
-            for h in range(NH):
-                cols = slice(h * B, (h + 1) * B)
-                dp = dot(values, r.dam[cols], NT)
-                ds = (r.e[i, j, :, cols].astype(F32) * (dp - deltas[h])).astype(BF)
-                r.ds[:, cols] = ds
-                part = slice(h * HEAD_DIM, (h + 1) * HEAD_DIM)
-                r.att[part] += dot(r.kt[part, kr], ds, NN)
-            r.dk[kr] += dot(r.ds[...], r.qm[i], NN)
-            r.dv[kr] += dot(r.e[i, j], r.dam[...], NN)
+        attend_back(0, s)
+        return 0
+
+    lax.fori_loop(0, 4, pair_step, 0)
+    round_kv(0)
+    grad_tiles(r.h1, r.dqa, r.gwa)
+    gr_start(PAIR)
+
+    def upper_back():
+        rs_m(3, 1).wait_recv()
+        for ch in range(CHUNKS):
+            rs_y(3, ch).wait_recv()
+
+        def finish_up(s, _):
+            at = rows(s * STEP, STEP)
+            r.made[0, at] = (r.res[at] + rs_total(3, at) + r.vecs[5:6]).astype(BF)
             return 0
 
-        lax.fori_loop(0, i + 1, over_keys, 0)
-        dq = (r.att[...].T * HEAD_DIM ** (-0.5)).astype(BF)
-        r.dqkv[0, at] = dq
+        lax.fori_loop(0, B // STEP, finish_up, 0)
+        if inside:
+            for k in range(1, n):
+                a2a_out_copy(0, k).start()
+            r.back0[hi] = r.made[0, rows(hi * PR, PR)]
+        else:
+            r.out_y_v[...] = r.made[0]
+
+    def last_step(s, _):
+        attend_back(1, s)
+
+        @pl.when(s == 1)
+        def _():
+            gr_mid(FC)
+
+        @pl.when(s == 2)
+        def _():
+            upper_back()
+
         return 0
 
-    lax.fori_loop(0, 4, attend_back, 0)
-
-    def round_kv(b, _):
-        at = rows(b * B, B)
-        dv = r.dv[at].astype(BF)
-        r.dqkv[1, at] = r.dk[at].astype(BF)
-        r.dqkv[2, at] = dv
-        r.acc_h[0] += fold(r.dqkv[0, at].astype(F32))
-        r.acc_h[1] += fold(dv.astype(F32))
-        return 0
-
-    lax.fori_loop(0, 4, round_kv, 0)
+    lax.fori_loop(0, 4, last_step, 0)
+    round_kv(1)
+    gr_mid(OUT)
 
     def lower(s, _):
         k = 3 - s
         at = block_rows(k)
-        part = dot(r.dqkv[0, at], r.wqkv[0], NT)
-        part = part + dot(r.dqkv[1, at], r.wqkv[1], NT)
-        part = part + dot(r.dqkv[2, at], r.wqkv[2], NT)
+        part = dot(r.dqa[at], r.wa[...], NT) + dot(r.dqb[at], r.wb[...], NT)
 
         @pl.when(s == 0)
         def _():
@@ -844,32 +995,11 @@
 
     lax.fori_loop(0, 4, lower, 0)
 
-    def grad_qkv(i, _):
-        at = rows(i * 256, 256)
-        left = r.h1[:, at]
-        for j in range(3):
-            r.gwqkv[j, at] = dot(left, r.dqkv[j], TN).astype(BF)
-        return 0
-
-    lax.fori_loop(0, D // 256, grad_qkv, 0)
-    gr_start(QKV)
-
-    rs_m(3, 1).wait_recv()
-    for ch in range(CHUNKS):
-        rs_y(3, ch).wait_recv()
-
-    def finish_up(s, _):
-        at = rows(s * STEP, STEP)
-        r.made[0, at] = (r.res[at] + rs_total(3, at) + r.vecs[5:6]).astype(BF)
-        return 0
-
-    lax.fori_loop(0, B // STEP, finish_up, 0)
-    if inside:
-        for k in range(1, n):
-            a2a_out_copy(0, k).start()
-        r.back0[hi] = r.made[0, rows(hi * PR, PR)]
-    else:
-        r.out_y_v[...] = r.made[0]
+    grad_tiles(r.h1, r.dqb, r.gwb)
+    gr_start(LAST)
+    gr_mid(PAIR)
+    gr_far(FC)
+    gr_far(OUT)
 
     def line(value):
         return jnp.sum(value, axis=0, keepdims=True)
@@ -878,11 +1008,16 @@
         spread(0, 8 * j, line(r.acc[at]))
     spread(0, 32, line(r.acc_f[...]))
     pad = jnp.zeros((1, 256 - HC), F32)
+    pair, last = line(r.acc_a[...]), line(r.acc_b[...])
     for j in range(2):
-        spread(0, 40 + 2 * j, jnp.concatenate([line(r.acc_h[j]), pad], axis=1))
+        spread(0, 40 + 2 * j, pair[:, 2 * j * PW : (2 * j + 1) * PW])
+        r.slab0[t, 41 + 2 * j : 42 + 2 * j, :LW] = last[:, 2 * j * LW : (2 * j + 1) * LW]
     sm_start(0)
 
     rs_m(2, 1).wait_recv()
+    sm_mid(0)
+    gr_far(PAIR)
+    gr_mid(LAST)
     for ch in range(CHUNKS):
         rs_y(2, ch).wait_recv()
 
@@ -904,10 +1039,8 @@
     for j in range(2):
         spread(1, 8 * j, line(r.acc[j]))
     sm_start(1)
-    sm_mid(0)
-    gr_mid(QKV)
-    gr_mid(OUT)
     sm_mid(1)
+    gr_far(LAST)
 
     OUTS = tuple(outputs(cfg))
 
@@ -942,7 +1075,12 @@
     store(OUT_X).start()
     r.out_late_v[...] = sm_finish(1)
     store(OUT_LATE).start()
-    r.out_qkv_v[...] = gr_finish(QKV)
+    total = gr_finish(PAIR)
+    for i in range(3):
+        r.out_qkv_v[i, :, :PW] = total[:, i * PW : (i + 1) * PW]
+    total = gr_finish(LAST)
+    for i in range(3):
+        r.out_qkv_v[i, :, PW:] = total[:, i * LW : (i + 1) * LW]
     store(OUT_QKV).start()
 
     for name in WG:
@@ -1019,6 +1157,8 @@
 def scratch(cfg):
     (n, packs, L, S, D, HC, FH, inside) = cfg
     NH = HC // HEAD_DIM
+    LW = HEAD_DIM
+    PW = HC - LW
     NZ = n // 2
     WR = D // n
     V = pltpu.VMEM
@@ -1029,7 +1169,8 @@
     made = Refs(
         came=V((2, L, D), BF),
         made=V((2, L, D), BF),
-        wqkv=V((3, D, HC), BF),
+        wa=V((D, 3 * PW), BF),
+        wb=V((D, 3 * LW), BF),
         wo=V((D, HC), BF),
         w1=V((D, FH), BF),
         w2=V((D, FH), BF),
@@ -1053,27 +1194,36 @@
         scale2=V((L, 1), F32),
         res=V((L, D), F32),
         dres=V((L, D), F32),
-        qm=V((blocks, NH * L, HC), BF),
-        k=V((S, HC), BF),
-        v=V((S, HC), BF),
+        qa=V((blocks, (NH - 1) * L, PW), BF),
+        ka=V((S, PW), BF),
+        va=V((S, PW), BF),
+        qb=V((blocks, L, LW), BF),
+        kb=V((S, LW), BF),
+        vb=V((S, LW), BF),
+        vbt=V((LW, 1), F32),
         kt=V((HC, S), BF),
         vt=V((HC, S), BF),
-        score=V((blocks, L, NH * L), F32),
-        e=V((blocks, blocks, L, NH * L), BF),
+        score=V((S, NH * L), F32),
+        e=V((blocks, S, NH * L), BF),
         att=V((HC, L), F32),
         inv=V((blocks, 8, L), F32),
         a=V((S, HC), F32),
         al=V((S, HC), BF),
-        dam=V((NH * L, HC), BF),
-        ds=V((L, NH * L), BF),
-        dk=V((S, HC), F32),
-        dv=V((S, HC), F32),
-        dqkv=V((3, S, HC), BF),
+        dama=V(((NH - 1) * L, PW), BF),
+        damb=V((L, LW), BF),
+        ds=V((2 * L, NH * L), BF),
+        dka=V((S, PW), F32),
+        dva=V((S, PW), F32),
+        dkb=V((S, LW), F32),
+        dvb=V((S, LW), F32),
+        dqa=V((S, 3 * PW), BF),
+        dqb=V((S, 3 * LW), BF),
         zz=V((S, FH), BF),
         du=V((S, FH), BF),
         acc=V((6, 8, D), F32),
         acc_f=V((8, FH), F32),
-        acc_h=V((2, 8, HC), F32),
+        acc_a=V((8, 3 * PW), F32),
+        acc_b=V((8, 3 * LW), F32),
         slab0=V((4, 48, 128), F32),
         slab1=V((4, 16, 128), F32),
         hslab0=V((n, 48, 128), F32),
@@ -1094,14 +1244,15 @@
         made["keep" + late] = V((2, L, D), F32)
         made["ys" + late] = V((L, D), BF)
         made["yr" + late] = V((L, D), BF)
-    for name, slot in ((QKV, (3, WR, HC)), (OUT, (WR, HC)), (FC, (WR, FH)), (PROJ, (WR, FH))):
+    for name, width in ((PAIR, 3 * PW), (LAST, 3 * LW), (OUT, HC), (FC, FH), (PROJ, FH)):
+        slot = (WR, width)
         made["g" + name] = V(slot[:-2] + (D, slot[-1]), BF)
         made[name + "_xr"] = V((NZ,) + slot, BF)
         made[name + "_zs"] = V((NZ - 1,) + slot, BF)
-        made[name + "_zr"] = V((NZ - 1,) + slot, BF)
+        made[name + "_zr"] = V((NZ,) + slot, BF)
     made.update(
-        wg_sem=sem((2, 4, 2 * NZ)),
-        gr_sem=sem((2, 4, 2 * NZ)),
+        wg_sem=sem((2, 5, 2 * NZ)),
+        gr_sem=sem((2, 5, 2 * NZ + 1)),
         ag_sem=sem((2, 4, 3, CHUNKS)),
         rs_sem=sem((2, 4, 2 + CHUNKS)),
         sm_sem=sem((2, 2, 3 + n)),

time: 175 us -> 163 us (0.931)
  Pallas kernels: 174 us -> 162 us
    pallas_call x1, Pallas kernels: 172 us -> 159 us  [local(): pl.pallas_call(functools.partial(kernel, cfg), out_shape=[jax.ShapeDtypeS...]
where the time goes in v3:
time: 163 us; the launch traced here: 162 us
  Pallas kernels  162 us (99%)
    pallas_call x1, Pallas kernels, local(): pl.pallas_call(functools.partial(kernel, cfg), out_shape=[jax.ShapeDtypeS...  159 us

profile of v3, /device:TPU:0, one launch (start us, length us, event | category | flops | bytes accessed | tf_op | source)
XLA Modules:
  0.0 162.4 jit_solution(7012577924622967836)
XLA Ops:
  0.7 159.0 %shard_map.263 = (bf16[8,32,768]{2,1,0:T(8,128)(2,1)}, bf16[8,32,768]{2,1,0:T(8,128)(2,1)}, f32[3,96,192]{2,1,0:T(8,128)}, f32[192,96]{1,0:T(8,128)}, f32[96,768...) custom-call(s32[8]{0:T(128)} %refs_0_.1, s32[4,8]{1,0:T(4,128)} %bitcast.36, ...), custom_call_target="tpu_custom_call" | custom-call | tf_op jit(solution)/shard_map/pallas_call | solution.py:1321
  159.7 2.7 %shard_map.264 = (bf16[256,768]{1,0:T(8,128)(2,1)}, bf16[256,768]{1,0:T(8,128)(2,1)}, f32[3,96,192]{2,1,0:T(8,128)}, f32[192,96]{1,0:T(8,128)}, f32[96,768]{1,0:...) custom-call(bf16[256,768]{1,0:T(8,128)(2,1)} %bitcast.23, ...), custom_call_target="tpu_custom_call" | custom-call | tf_op jit(solution)/shard_map/pallas_call | solution.py:1361

commit v4 on v3

--- a/solution.py
+++ b/solution.py
@@ -22,6 +22,8 @@
 
 PAIR, LAST, OUT, FC, PROJ = "wa", "wb", "wo", "w1", "w2"
 QKV = "wqkv"
+PROJ_Z, FC_Z = "w2z", "w1z"
+ZFIRST = (PROJ_Z, FC_Z)
 H1, GF, H2, DR = "h1", "gf", "h2", "dr"
 X_IN, G_IN = "x", "g"
 OUT_Y, OUT_X, OUT_QKV, OUT_WO = "out_y", "out_x", "out_qkv", "out_wo"
@@ -151,7 +153,7 @@
             r.vecs[j : j + 1, i * 128 : (i + 1) * 128] = vec[i : i + 1]
 
     WG = (PAIR, LAST, OUT, FC, PROJ)
-    STRAIGHT = (PAIR, LAST, OUT)
+    STRAIGHT = (PAIR, LAST)
     middle = (z == 1) | (z == 2)
     side = z // 2
     near, far_mid, far_end = z + 1 - 2 * (z % 2), 2 - side, 3 - 3 * side
@@ -190,16 +192,11 @@
         slot = wslot(name, r[name], 2 * (Z_FROM + (z,))[i] + xx)
         return rcopy(slot, slot, sem.at[0, a, 4 + i], sem.at[1, a, 4 + i], xnb)
 
-    def wg_start(name):
-        wg_z(name, 0).start()
-        wg_z(name, 1).start()
-
-    def wg_first(name):
+    def wg_near(name):
         wg_in(name, 0).wait_recv()
         wg_x(name, 0).start()
-        if name in STRAIGHT:
-            return
-
+
+    def wg_mids(name):
         @pl.when(middle)
         def _():
             for i in (1, 2):
@@ -347,33 +344,68 @@
         for ch in range(CHUNKS):
             rs_y(tag, ch).wait_send()
 
-    GR = {name: "g" + name for name in WG}
+    GS = WG + ZFIRST
+    GR = {name: "g" + name for name in GS}
+    HF = FH // 2
 
     def gr_x(name, k):
         sem = r.gr_sem
-        a = WG.index(name)
+        a = GS.index(name)
         slot = wslot(name, r[GR[name]], 2 * k + 1 - xx)
         return rcopy(slot, r[name + "_xr"].at[k], sem.at[0, a, k], sem.at[1, a, k], xnb)
 
     def gr_z(name, i):
         sem = r.gr_sem
-        a = WG.index(name)
+        a = GS.index(name)
         to_mid, to_end = dev(2 * far_mid + xx, t), dev(2 * far_end + xx, t)
-        if name == PROJ:
+        if name in ZFIRST:
             to, source = (near_dev, to_mid, to_end)[i], i
             recv = 0 if i == 0 else jnp.where(middle, 1, 2)
         else:
             to = {0: near_dev, 2: near_dev, 3: near_dev, 1: to_mid, 4: to_end}[i]
             source = {0: 0, 2: 1, 3: 2, 1: 1, 4: 2}[i]
             recv = 1 if i == 4 else i
-        part = r[name + "_zs"].at[source]
+        part = two(name, Z_FROM[source]) if name in ZFIRST else r[name + "_zs"].at[source]
         return rcopy(part, r[name + "_zr"].at[recv], sem.at[0, a, NZ + i], sem.at[1, a, NZ + recv], to)
 
     def gr_zin(name, i):
         sem = r.gr_sem
-        a = WG.index(name)
+        a = GS.index(name)
         part = r[name + "_zr"].at[i]
         return rcopy(part, part, sem.at[0, a, NZ], sem.at[1, a, NZ + i], near_dev)
+
+    def two(name, place):
+        return r[GR[name]].at[rows(2 * place * WR, 2 * WR, 32)]
+
+    def z_start(name):
+        for i in range(3):
+            gr_z(name, i).start()
+
+    def x_last(name):
+        sem = r.gr_sem
+        a = GS.index(name)
+        return rcopy(r[name + "_xs"], r[name + "_xr"], sem.at[0, a, 0], sem.at[1, a, 0], xnb)
+
+    def z_end(name, out):
+        zr = r[name + "_zr"]
+        came = range(3)
+        for i in came:
+            gr_zin(name, i).wait_recv()
+
+        def total(k):
+            value = r[GR[name]][rows((2 * z + k) * WR, WR, 16)].astype(F32)
+            at = rows(k * WR, WR, 16)
+            for i in came:
+                value = value + zr[i, at].astype(F32)
+            return value
+
+        r[name + "_xs"][...] = total(1 - xx).astype(BF)
+        x_last(name).start()
+        out[:, HF:] = total(xx)
+
+    def z_finish(name, out):
+        x_last(name).wait_recv()
+        out[:, HF:] += r[name + "_xr"][...].astype(F32)
 
     def gr_start(name):
         for k in range(NZ):
@@ -389,11 +421,6 @@
         zs = r[name + "_zs"]
         zs[0] = gr_pair(name, near).astype(BF)
         gr_z(name, 0).start()
-        if name == PROJ:
-            for i in (1, 2):
-                zs[i] = gr_pair(name, Z_FROM[i]).astype(BF)
-                gr_z(name, i).start()
-            return
 
         @pl.when(jnp.logical_not(middle))
         def _():
@@ -415,16 +442,19 @@
 
     def gr_finish(name):
         total = gr_pair(name, z)
-        for i in range(3 if name == PROJ else 2):
+        for i in range(2):
             gr_zin(name, i).wait_recv()
             total = total + r[name + "_zr"][i].astype(F32)
         return total
 
     def gr_drain(name):
-        for k in range(NZ):
-            gr_x(name, k).wait_send()
+        if name in ZFIRST:
+            x_last(name).wait_send()
+        else:
+            for k in range(NZ):
+                gr_x(name, k).wait_send()
         gr_z(name, 0).wait_send()
-        if name == PROJ:
+        if name in ZFIRST:
             gr_z(name, 1).wait_send()
             gr_z(name, 2).wait_send()
             return
@@ -470,7 +500,7 @@
         if tag == 0:
             keep = lax.broadcasted_iota(jnp.int32, total.shape, 0) < SHARED[0]
             total = jnp.where(keep, total, slab[t])
-        hslab[hi] = total
+        hslab[hi] = total.astype(BF)
         for k in range(1, n):
             sm_h(tag, k).start()
 
@@ -478,9 +508,9 @@
         for k in range(1, n):
             sm_h(tag, k).wait_recv()
         hslab = hslabs[tag]
-        total = hslab[0]
+        total = hslab[0].astype(F32)
         for k in range(1, n):
-            total = total + hslab[k]
+            total = total + hslab[k].astype(F32)
         return total
 
     def sm_drain(tag):
@@ -505,6 +535,7 @@
     for name in STRAIGHT:
         wg_z(name, 1).start()
         wg_z(name, 2).start()
+    wg_z(FC, 0).start()
 
     def norm_step(values, at, gain, bias, cen, scale):
         mean = jnp.mean(values, axis=1, keepdims=True)
@@ -539,19 +570,22 @@
         lax.fori_loop(0, CR // STEP, one, 0)
         ag_send(H1, ch)
 
-    for name in STRAIGHT:
-        wg_first(name)
+    for name in (PAIR, LAST, OUT):
+        wg_near(name)
     wg_second(PAIR)
+    wg_z(OUT, 1).start()
     ag_arrive(H1, 1)
     ag_arrive(H1, 2)
     wg_second(LAST)
-    wg_second(OUT)
     if inside:
         for k in range(1, n):
             a2a_in_copy(1, k).start()
-    wg_start(FC)
     wg_wait(PAIR)
     wg_wait(LAST)
+    wg_mids(OUT)
+    wg_near(FC)
+    wg_z(FC, 1).start()
+    wg_z(PROJ, 0).start()
 
     lane = lax.broadcasted_iota(jnp.int32, (1, PW), 1)
 
@@ -592,7 +626,9 @@
     bias_last = jnp.concatenate([r.qvb[1:2, PW:], jnp.zeros((1, LW), F32)], axis=1)
     r.vbt[...] = jnp.broadcast_to(bias_last, (8, 2 * LW)).T[:LW, :1]
     lax.fori_loop(0, 4, project, 0)
-    wg_start(PROJ)
+    wg_second(OUT)
+    wg_near(PROJ)
+    wg_z(PROJ, 1).start()
 
     def own_grad(s, _):
         at = rows(s * STEP, STEP)
@@ -679,7 +715,6 @@
         def _():
             rs_put(0, 3, part)
             rs_m(0, 0).start()
-            grad_in()
 
         @pl.when(s == 1)
         def _():
@@ -690,7 +725,7 @@
         def _():
             rs_put(0, 1, part)
             rs_m(0, 1).start()
-            wg_first(FC)
+            wg_mids(PROJ)
 
         @pl.when(s == 3)
         def _():
@@ -698,14 +733,15 @@
 
         return 0
 
+    grad_in()
+    wg_mids(FC)
     lax.fori_loop(0, 4, attend_step, 0)
     wg_second(FC)
-    ag_arrive(GF, 1)
-    ag_arrive(GF, 2)
-    wg_first(PROJ)
 
     rs_m(0, 1).wait_recv()
     for ch in range(CHUNKS):
+        if ch == CHUNKS - 1:
+            wg_second(PROJ)
         rs_y(0, ch).wait_recv()
 
         def one(s, _):
@@ -720,22 +756,23 @@
         lax.fori_loop(0, CR // STEP, one, 0)
         ag_send(H2, ch)
     rs_drain(0)
-    wg_second(PROJ)
-    ag_arrive(GF, 3)
     wg_wait(FC)
     wg_wait(PROJ)
 
     def feed(s, _):
         @pl.when(s == 1)
         def _():
+            ag_arrive(GF, 1)
             ag_arrive(H2, 1)
 
         @pl.when(s == 2)
         def _():
+            ag_arrive(GF, 2)
             ag_arrive(H2, 2)
 
         @pl.when(s == 3)
         def _():
+            ag_arrive(GF, 3)
             ag_arrive(H2, 3)
 
         at = block_rows(s)
@@ -778,17 +815,22 @@
     lax.fori_loop(0, 4, feed, 0)
     rs_ship(1)
 
-    def grad_tiles(left, right, out, form=TN):
+    def grad_tiles(left, right, out, cols=slice(None)):
         def one(i, _):
             at = rows(i * 256, 256)
-            out[at] = dot(left[:, at], right[...], form).astype(BF)
+            out[at] = dot(left[:, at], right[:, cols], TN).astype(BF)
             return 0
 
         lax.fori_loop(0, D // 256, one, 0)
 
-    grad_tiles(r.gf, r.zz, r.gw2)
+    grad_tiles(r.gf, r.zz, r.gw2z, slice(HF, FH))
+    z_start(PROJ_Z)
+    grad_tiles(r.gf, r.zz, r.gw2, slice(0, HF))
     gr_start(PROJ)
-    grad_tiles(r.h2, r.du, r.gw1)
+    grad_tiles(r.h2, r.du, r.gw1z, slice(HF, FH))
+    z_start(FC_Z)
+    grad_tiles(r.h2, r.du, r.gw1, slice(0, HF))
+    gr_start(FC)
 
     rs_m(1, 1).wait_recv()
     for ch in range(CHUNKS):
@@ -832,67 +874,67 @@
         return 0
 
     lax.fori_loop(0, 4, upper, 0)
-    gr_start(FC)
-
-    PASS = (
-        (0, PW, NH - 1, r.qa, r.ka, r.va, r.dama, r.dka, r.dva, r.dqa),
-        (PW, LW, 1, r.qb, r.kb, r.vb, r.damb, r.dkb, r.dvb, r.dqb),
-    )
-
-    def attend_back(which, s):
-        first, width, heads, q, k, v, dam, dk, dv, dqkv = PASS[which]
-        cols = slice(first, first + width)
-        i = block_of(s)
+
+    lanes = lax.broadcasted_iota(jnp.int32, (1, HC), 1)
+    LB = (NH - 1) * B
+
+    def attend_back(i):
         at = rows(i * B, B)
-        da = dot(r.dr[at], r.wo[:, cols], NN).astype(BF).astype(F32)
+        da = dot(r.dr[at], r.wo[...], NN).astype(BF).astype(F32)
         by_row = r.inv[i].T
-        if which == 0:
-            scale = by_row[:, heads - 1 : heads]
-            for h in range(heads - 1):
-                scale = jnp.where(head_mask(h), by_row[:, h : h + 1], scale)
-        else:
-            scale = by_row[:, NH - 1 : NH]
+        scale = by_row[:, NH - 1 : NH]
+        for h in range(NH - 1):
+            scale = jnp.where(lanes // HEAD_DIM == h, by_row[:, h : h + 1], scale)
         low = (da * scale).astype(BF)
-        for h in range(heads):
-            dam[h * B : (h + 1) * B] = (
-                jnp.where(head_mask(h), low, jnp.zeros_like(low)) if which == 0 else low
-            )
-        if which == 0:
-            lined = (low.astype(F32) * r.a[at, :PW]).T
-        else:
-            both = low.astype(F32) * r.a[at, PW:]
-            lined = jnp.concatenate([both, both], axis=1).T
+        pair = low[:, :PW]
+        for h in range(NH - 1):
+            r.dama[h * B : (h + 1) * B] = jnp.where(head_mask(h), pair, jnp.zeros_like(pair))
+        r.damb[at] = low[:, PW:]
+        lined = (low.astype(F32) * r.a[at]).T
         deltas = [
             jnp.sum(lined[h * HEAD_DIM : (h + 1) * HEAD_DIM], axis=0, keepdims=True)
-            for h in range(heads)
+            for h in range(NH)
         ]
-        r.att[cols] = jnp.zeros((width, B), F32)
+        r.inv[i, 4:5] = deltas[NH - 1]
+        r.att[:PW] = jnp.zeros((PW, B), F32)
 
         def over_keys(j, _):
             kr = rows(j * KB, KB)
-            values = v[kr]
-            base = first // HEAD_DIM * B
-            for h in range(heads):
+            values = r.va[kr]
+            for h in range(NH - 1):
                 own = slice(h * B, (h + 1) * B)
-                dp = dot(values, dam[own], NT)
-                weight = r.e[i, kr, base + h * B : base + (h + 1) * B]
-                ds = (weight.astype(F32) * (dp - deltas[h])).astype(BF)
+                dp = dot(values, r.dama[own], NT)
+                ds = (r.e[i, kr, own].astype(F32) * (dp - deltas[h])).astype(BF)
                 r.ds[:, own] = ds
-                part = slice(first + h * HEAD_DIM, first + (h + 1) * HEAD_DIM)
+                part = slice(h * HEAD_DIM, (h + 1) * HEAD_DIM)
                 r.att[part] += dot(r.kt[part, kr], ds, NN)
-            dk[kr] += dot(r.ds[:, : heads * B], q[i], NN)
-            dv[kr] += dot(r.e[i, kr, base : base + heads * B], dam[...], NN)
+            r.dka[kr] += dot(r.ds[...], r.qa[i], NN)
+            r.dva[kr] += dot(r.e[i, kr, :LB], r.dama[...], NN)
             return 0
 
         lax.fori_loop(0, (i + KS) // KS, over_keys, 0)
-        if which == 0:
-            dq = r.att[cols].T
-        else:
-            dq = jnp.concatenate([r.att[cols], r.att[cols]], axis=0).T[:, :width]
-        dqkv[at, :width] = (dq * HEAD_DIM ** (-0.5)).astype(BF)
+        r.dqa[at, :PW] = (r.att[:PW].T * HEAD_DIM ** (-0.5)).astype(BF)
+
+    def attend_back_last():
+        blocks = S // B
+        for i in reversed(range(blocks)):
+            at, keys = slice(i * B, (i + 1) * B), slice(0, (i + 1) * B)
+            grad = r.damb[at]
+            dp = dot(r.vb[keys], grad, NT)
+            weight = r.e[i, keys, LB:]
+            ds = (weight.astype(F32) * (dp - r.inv[i, 4:5])).astype(BF)
+            dq = dot(r.kt[PW:, keys], ds, NN)
+            dk, dv = dot(ds, r.qb[i], NN), dot(weight, grad, NN)
+            if i == blocks - 1:
+                r.dkb[...], r.dvb[...] = dk, dv
+            else:
+                r.dkb[keys] += dk
+                r.dvb[keys] += dv
+            dq = jnp.concatenate([dq, dq], axis=0).T[:, :LW]
+            r.dqb[at, :LW] = (dq * HEAD_DIM ** (-0.5)).astype(BF)
 
     def round_kv(which):
-        first, width, _, _, _, _, _, dk, dv, dqkv = PASS[which]
+        width, dk, dv, dqkv = ((PW, r.dka, r.dva, r.dqa), (LW, r.dkb, r.dvb, r.dqb))[which]
 
         def one(b, _):
             at = rows(b * B, B)
@@ -904,7 +946,7 @@
 
         lax.fori_loop(0, 4, one, 0)
 
-    for zeroed in (r.dka, r.dva, r.dkb, r.dvb):
+    for zeroed in (r.dka, r.dva):
         zeroed[...] = jnp.zeros_like(zeroed)
 
     def pair_step(s, _):
@@ -921,16 +963,19 @@
         @pl.when(s == 3)
         def _():
             ag_arrive(DR, 3)
+            gr_mid(FC)
             grad_tiles(r.dr, r.al, r.gwo)
             gr_start(OUT)
 
-        attend_back(0, s)
+        attend_back(block_of(s))
         return 0
 
     lax.fori_loop(0, 4, pair_step, 0)
     round_kv(0)
     grad_tiles(r.h1, r.dqa, r.gwa)
     gr_start(PAIR)
+    gr_far(PROJ)
+    z_end(PROJ_Z, r.out_w2_v)
 
     def upper_back():
         rs_m(3, 1).wait_recv()
@@ -950,20 +995,7 @@
         else:
             r.out_y_v[...] = r.made[0]
 
-    def last_step(s, _):
-        attend_back(1, s)
-
-        @pl.when(s == 1)
-        def _():
-            gr_mid(FC)
-
-        @pl.when(s == 2)
-        def _():
-            upper_back()
-
-        return 0
-
-    lax.fori_loop(0, 4, last_step, 0)
+    attend_back_last()
     round_kv(1)
     gr_mid(OUT)
 
@@ -997,8 +1029,9 @@
 
     grad_tiles(r.h1, r.dqb, r.gwb)
     gr_start(LAST)
-    gr_mid(PAIR)
+    upper_back()
     gr_far(FC)
+    z_end(FC_Z, r.out_w1_v)
     gr_far(OUT)
 
     def line(value):
@@ -1013,12 +1046,12 @@
         spread(0, 40 + 2 * j, pair[:, 2 * j * PW : (2 * j + 1) * PW])
         r.slab0[t, 41 + 2 * j : 42 + 2 * j, :LW] = last[:, 2 * j * LW : (2 * j + 1) * LW]
     sm_start(0)
+    gr_mid(PAIR)
 
     rs_m(2, 1).wait_recv()
-    sm_mid(0)
-    gr_far(PAIR)
-    gr_mid(LAST)
     for ch in range(CHUNKS):
+        if ch == CHUNKS - 1:
+            sm_mid(0)
         rs_y(2, ch).wait_recv()
 
         def one(s, _):
@@ -1039,6 +1072,8 @@
     for j in range(2):
         spread(1, 8 * j, line(r.acc[j]))
     sm_start(1)
+    gr_mid(LAST)
+    gr_far(PAIR)
     sm_mid(1)
     gr_far(LAST)
 
@@ -1057,9 +1092,11 @@
 
         lax.fori_loop(0, n, one, 0)
 
-    r.out_w2_v[...] = gr_finish(PROJ)
+    z_finish(PROJ_Z, r.out_w2_v)
+    r.out_w2_v[:, :HF] = gr_finish(PROJ)
     store(OUT_W2).start()
-    r.out_w1_v[...] = gr_finish(FC)
+    z_finish(FC_Z, r.out_w1_v)
+    r.out_w1_v[:, :HF] = gr_finish(FC)
     store(OUT_W1).start()
     if inside:
         put_back(0, r.out_y_v)
@@ -1085,6 +1122,7 @@
 
     for name in WG:
         wg_drain(name)
+    for name in GS:
         gr_drain(name)
     for name in AG:
         ag_drain(name)
@@ -1210,8 +1248,8 @@
         a=V((S, HC), F32),
         al=V((S, HC), BF),
         dama=V(((NH - 1) * L, PW), BF),
-        damb=V((L, LW), BF),
-        ds=V((2 * L, NH * L), BF),
+        damb=V((S, LW), BF),
+        ds=V((2 * L, (NH - 1) * L), BF),
         dka=V((S, PW), F32),
         dva=V((S, PW), F32),
         dkb=V((S, LW), F32),
@@ -1226,8 +1264,8 @@
         acc_b=V((8, 3 * LW), F32),
         slab0=V((4, 48, 128), F32),
         slab1=V((4, 16, 128), F32),
-        hslab0=V((n, 48, 128), F32),
-        hslab1=V((n, 16, 128), F32),
+        hslab0=V((n, 48, 128), BF),
+        hslab1=V((n, 16, 128), BF),
     )
     for name, (shape, dtype) in outputs(cfg).items():
         made[name + "_v"] = V(shape, dtype)
@@ -1244,15 +1282,20 @@
         made["keep" + late] = V((2, L, D), F32)
         made["ys" + late] = V((L, D), BF)
         made["yr" + late] = V((L, D), BF)
-    for name, width in ((PAIR, 3 * PW), (LAST, 3 * LW), (OUT, HC), (FC, FH), (PROJ, FH)):
+    for name, width in ((PAIR, 3 * PW), (LAST, 3 * LW), (OUT, HC)) + tuple((name, FH // 2) for name in (FC, PROJ) + ZFIRST):
         slot = (WR, width)
-        made["g" + name] = V(slot[:-2] + (D, slot[-1]), BF)
+        made["g" + name] = V((D, width), BF)
+        if name in ZFIRST:
+            made[name + "_xs"] = V(slot, BF)
+            made[name + "_xr"] = V(slot, BF)
+            made[name + "_zr"] = V((3, 2 * WR, width), BF)
+            continue
         made[name + "_xr"] = V((NZ,) + slot, BF)
         made[name + "_zs"] = V((NZ - 1,) + slot, BF)
         made[name + "_zr"] = V((NZ,) + slot, BF)
     made.update(
         wg_sem=sem((2, 5, 2 * NZ)),
-        gr_sem=sem((2, 5, 2 * NZ + 1)),
+        gr_sem=sem((2, 7, 2 * NZ + 1)),
         ag_sem=sem((2, 4, 3, CHUNKS)),
         rs_sem=sem((2, 4, 2 + CHUNKS)),
         sm_sem=sem((2, 2, 3 + n)),

time: 163 us -> 151 us (0.926)
  Pallas kernels: 162 us -> 150 us
    pallas_call x1, Pallas kernels: 159 us -> 148 us  [local(): pl.pallas_call(functools.partial(kernel, cfg), out_shape=[jax.ShapeDtypeS...]
where the time goes in v4:
time: 151 us
  Pallas kernels  150 us (99%)
    pallas_call x1, Pallas kernels, local(): pl.pallas_call(functools.partial(kernel, cfg), out_shape=[jax.ShapeDtypeS...  148 us

profile of v4, /device:TPU:0, one launch (start us, length us, event | category | flops | bytes accessed | tf_op | source)
XLA Modules:
  0.0 151.0 jit_solution(8904369225875635207)
XLA Ops:
  0.7 147.6 %shard_map.263 = (bf16[8,32,768]{2,1,0:T(8,128)(2,1)}, bf16[8,32,768]{2,1,0:T(8,128)(2,1)}, f32[3,96,192]{2,1,0:T(8,128)}, f32[192,96]{1,0:T(8,128)}, f32[96,768...) custom-call(s32[8]{0:T(128)} %refs_0_.1, s32[4,8]{1,0:T(4,128)} %bitcast.36, ...), custom_call_target="tpu_custom_call" | custom-call | tf_op jit(solution)/shard_map/pallas_call | solution.py:1364
  148.3 2.7 %shard_map.264 = (bf16[256,768]{1,0:T(8,128)(2,1)}, bf16[256,768]{1,0:T(8,128)(2,1)}, f32[3,96,192]{2,1,0:T(8,128)}, f32[192,96]{1,0:T(8,128)}, f32[96,768]{1,0:...) custom-call(bf16[256,768]{1,0:T(8,128)(2,1)} %bitcast.23, ...), custom_call_target="tpu_custom_call" | custom-call | tf_op jit(solution)/shard_map/pallas_call | solution.py:1404

commit v5 on v4

--- a/solution.py
+++ b/solution.py
@@ -306,10 +306,13 @@
         sem = r.rs_sem
         return rcopy(ms.at[i], mr.at[i], sem.at[0, tag, i], sem.at[1, tag, i], mate)
 
+    def chunk_at(tag, ch):
+        return (1 - side + ch) % CHUNKS * CR if tag == 2 else ch * CR
+
     def rs_y(tag, ch):
         _, _, _, ys, yr = rs_bufs(tag)
         sem = r.rs_sem
-        where = pl.ds(ch * CR, CR)
+        where = rows(chunk_at(tag, ch), CR)
         return rcopy(ys.at[where], yr.at[where], sem.at[0, tag, 2 + ch], sem.at[1, tag, 2 + ch], ynb)
 
     def rs_put(tag, k, value, at=None):
@@ -327,7 +330,7 @@
         for ch in range(CHUNKS):
 
             def one(s, _):
-                at = rows(ch * CR + s * STEP, STEP)
+                at = rows(chunk_at(tag, ch) + s * STEP, STEP)
                 ys[at] = (keep[0, at] + mr[0, at].astype(F32)).astype(BF)
                 return 0
 
@@ -715,6 +718,7 @@
         def _():
             rs_put(0, 3, part)
             rs_m(0, 0).start()
+            wg_mids(FC)
 
         @pl.when(s == 1)
         def _():
@@ -734,7 +738,6 @@
         return 0
 
     grad_in()
-    wg_mids(FC)
     lax.fori_loop(0, 4, attend_step, 0)
     wg_second(FC)
 
@@ -998,6 +1001,7 @@
     attend_back_last()
     round_kv(1)
     gr_mid(OUT)
+    upper_back()
 
     def lower(s, _):
         k = 3 - s
@@ -1029,7 +1033,6 @@
 
     grad_tiles(r.h1, r.dqb, r.gwb)
     gr_start(LAST)
-    upper_back()
     gr_far(FC)
     z_end(FC_Z, r.out_w1_v)
     gr_far(OUT)
@@ -1055,17 +1058,28 @@
         rs_y(2, ch).wait_recv()
 
         def one(s, _):
-            at = rows(ch * CR + s * STEP, STEP)
+            at = rows(chunk_at(2, ch) + s * STEP, STEP)
             back = norm_back(rs_total(2, at), at, r.vecs[0:1], r.cen1, r.scale1, 0)
             r.made[1, at] = (r.dres[at] + back).astype(BF)
             return 0
 
         lax.fori_loop(0, CR // STEP, one, 0)
+        if inside:
+
+            def send(j, _):
+                to = chunk_at(2, ch) // PR + j
+
+                @pl.when(to != hi)
+                def _():
+                    a2a_out_copy(1, (to - hi + n) % n).start()
+
+                return 0
+
+            lax.fori_loop(0, CR // PR, send, 0)
+
     rs_drain(2)
     rs_drain(3)
     if inside:
-        for k in range(1, n):
-            a2a_out_copy(1, k).start()
         r.back1[hi] = r.made[1, rows(hi * PR, PR)]
     else:
         r.out_x_v[...] = r.made[1]

time: 151 us -> 146 us (0.967)
  Pallas kernels: 150 us -> 145 us
    pallas_call x1, Pallas kernels: 148 us -> 142 us  [local(): pl.pallas_call(functools.partial(kernel, cfg), out_shape=[jax.ShapeDtypeS...]
where the time goes in v5:
time: 146 us; the launch traced here: 145 us
  Pallas kernels  145 us (99%)
    pallas_call x1, Pallas kernels, local(): pl.pallas_call(functools.partial(kernel, cfg), out_shape=[jax.ShapeDtypeS...  142 us

profile of v5, /device:TPU:0, one launch (start us, length us, event | category | flops | bytes accessed | tf_op | source)
XLA Modules:
  0.0 145.4 jit_solution(13899466926391420839)
XLA Ops:
  0.7 142.1 %shard_map.263 = (bf16[8,32,768]{2,1,0:T(8,128)(2,1)}, bf16[8,32,768]{2,1,0:T(8,128)(2,1)}, f32[3,96,192]{2,1,0:T(8,128)}, f32[192,96]{1,0:T(8,128)}, f32[96,768...) custom-call(s32[8]{0:T(128)} %refs_0_.1, s32[4,8]{1,0:T(4,128)} %bitcast.36, ...), custom_call_target="tpu_custom_call" | custom-call | tf_op jit(solution)/shard_map/pallas_call | solution.py:1378
  142.7 2.7 %shard_map.264 = (bf16[256,768]{1,0:T(8,128)(2,1)}, bf16[256,768]{1,0:T(8,128)(2,1)}, f32[3,96,192]{2,1,0:T(8,128)}, f32[192,96]{1,0:T(8,128)}, f32[96,768]{1,0:...) custom-call(bf16[256,768]{1,0:T(8,128)(2,1)} %bitcast.23, ...), custom_call_target="tpu_custom_call" | custom-call | tf_op jit(solution)/shard_map/pallas_call | solution.py:1418

commit v6 on v5

--- a/solution.py
+++ b/solution.py
@@ -153,7 +153,7 @@
             r.vecs[j : j + 1, i * 128 : (i + 1) * 128] = vec[i : i + 1]
 
     WG = (PAIR, LAST, OUT, FC, PROJ)
-    STRAIGHT = (PAIR, LAST)
+    STRAIGHT = (PAIR,)
     middle = (z == 1) | (z == 2)
     side = z // 2
     near, far_mid, far_end = z + 1 - 2 * (z % 2), 2 - side, 3 - 3 * side
@@ -162,6 +162,10 @@
 
     def wslot(name, ref, slot):
         return ref.at[rows(slot * WR, WR, 16)]
+
+    def gslot(name, slot):
+        high = WR // 2 if name in (LAST, OUT) else WR
+        return r[GR[name]].at[rows(slot * high, high, 16)]
 
     def wg_z(name, i):
         sem = r.wg_sem
@@ -354,7 +358,7 @@
     def gr_x(name, k):
         sem = r.gr_sem
         a = GS.index(name)
-        slot = wslot(name, r[GR[name]], 2 * k + 1 - xx)
+        slot = gslot(name, 2 * k + 1 - xx)
         return rcopy(slot, r[name + "_xr"].at[k], sem.at[0, a, k], sem.at[1, a, k], xnb)
 
     def gr_z(name, i):
@@ -415,7 +419,7 @@
             gr_x(name, k).start()
 
     def gr_pair(name, to):
-        mine = wslot(name, r[GR[name]], 2 * to + xx)[...].astype(F32)
+        mine = gslot(name, 2 * to + xx)[...].astype(F32)
         return mine + r[name + "_xr"][to].astype(F32)
 
     def gr_mid(name):
@@ -538,6 +542,7 @@
     for name in STRAIGHT:
         wg_z(name, 1).start()
         wg_z(name, 2).start()
+    wg_z(LAST, 1).start()
     wg_z(FC, 0).start()
 
     def norm_step(values, at, gain, bias, cen, scale):
@@ -576,6 +581,7 @@
     for name in (PAIR, LAST, OUT):
         wg_near(name)
     wg_second(PAIR)
+    wg_mids(LAST)
     wg_z(OUT, 1).start()
     ag_arrive(H1, 1)
     ag_arrive(H1, 2)
@@ -817,6 +823,19 @@
 
     lax.fori_loop(0, 4, feed, 0)
     rs_ship(1)
+
+    def grad_halves(left, right, out):
+        def one(i, _):
+            value = dot(left[:, rows(i * 384, 384)], right[...], TN)
+            for j in range(384 // WR):
+                first, second = (2 * j) * WR // 2, (2 * j + 1) * WR // 2
+                both = jnp.concatenate(
+                    [value[first : first + WR // 2], value[second : second + WR // 2]], axis=1
+                )
+                out[rows((i * (384 // WR) + j) * (WR // 2), WR // 2, 16)] = both.astype(BF)
+            return 0
+
+        lax.fori_loop(0, D // 384, one, 0)
 
     def grad_tiles(left, right, out, cols=slice(None)):
         def one(i, _):
@@ -967,7 +986,7 @@
         def _():
             ag_arrive(DR, 3)
             gr_mid(FC)
-            grad_tiles(r.dr, r.al, r.gwo)
+            grad_halves(r.dr, r.al, r.gwo)
             gr_start(OUT)
 
         attend_back(block_of(s))
@@ -1031,7 +1050,7 @@
 
     lax.fori_loop(0, 4, lower, 0)
 
-    grad_tiles(r.h1, r.dqb, r.gwb)
+    grad_halves(r.h1, r.dqb, r.gwb)
     gr_start(LAST)
     gr_far(FC)
     z_end(FC_Z, r.out_w1_v)
@@ -1116,7 +1135,9 @@
         put_back(0, r.out_y_v)
     store(OUT_Y).start()
     r.turn[...] = jnp.zeros_like(r.turn)
-    r.turn[:WR, :HC] = gr_finish(OUT)
+    packed = gr_finish(OUT)
+    r.turn[: WR // 2, :HC] = packed[:, :HC]
+    r.turn[WR // 2 : WR, :HC] = packed[:, HC:]
     r.out_wo_v[...] = r.turn[...].T[:HC, :WR]
     store(OUT_WO).start()
     r.out_early_v[...] = sm_finish(0)
@@ -1129,7 +1150,8 @@
     total = gr_finish(PAIR)
     for i in range(3):
         r.out_qkv_v[i, :, :PW] = total[:, i * PW : (i + 1) * PW]
-    total = gr_finish(LAST)
+    packed = gr_finish(LAST)
+    total = jnp.concatenate([packed[:, : 3 * LW], packed[:, 3 * LW :]], axis=0)
     for i in range(3):
         r.out_qkv_v[i, :, PW:] = total[:, i * LW : (i + 1) * LW]
     store(OUT_QKV).start()
@@ -1297,8 +1319,9 @@
         made["ys" + late] = V((L, D), BF)
         made["yr" + late] = V((L, D), BF)
     for name, width in ((PAIR, 3 * PW), (LAST, 3 * LW), (OUT, HC)) + tuple((name, FH // 2) for name in (FC, PROJ) + ZFIRST):
-        slot = (WR, width)
-        made["g" + name] = V((D, width), BF)
+        packed = 2 if name in (LAST, OUT) else 1
+        slot = (WR // packed, width * packed)
+        made["g" + name] = V((D // packed, width * packed), BF)
         if name in ZFIRST:
             made[name + "_xs"] = V(slot, BF)
             made[name + "_xr"] = V(slot, BF)

time: 146 us -> 143 us (0.979)
  Pallas kernels: 145 us -> 142 us
    pallas_call x1, Pallas kernels: 142 us -> 139 us  [local(): pl.pallas_call(functools.partial(kernel, cfg), out_shape=[jax.ShapeDtypeS...]
where the time goes in v6:
time: 143 us
  Pallas kernels  142 us (99%)
    pallas_call x1, Pallas kernels, local(): pl.pallas_call(functools.partial(kernel, cfg), out_shape=[jax.ShapeDtypeS...  139 us

profile of v6, /device:TPU:0, one launch (start us, length us, event | category | flops | bytes accessed | tf_op | source)
XLA Modules:
  0.0 142.8 jit_solution(17322247726331873884)
XLA Ops:
  0.7 139.3 %shard_map.263 = (bf16[8,32,768]{2,1,0:T(8,128)(2,1)}, bf16[8,32,768]{2,1,0:T(8,128)(2,1)}, f32[3,96,192]{2,1,0:T(8,128)}, f32[192,96]{1,0:T(8,128)}, f32[96,768...) custom-call(s32[8]{0:T(128)} %refs_0_.1, s32[4,8]{1,0:T(4,128)} %bitcast.36, ...), custom_call_target="tpu_custom_call" | custom-call | tf_op jit(solution)/shard_map/pallas_call | solution.py:1401
  140.0 2.7 %shard_map.264 = (bf16[256,768]{1,0:T(8,128)(2,1)}, bf16[256,768]{1,0:T(8,128)(2,1)}, f32[3,96,192]{2,1,0:T(8,128)}, f32[192,96]{1,0:T(8,128)}, f32[96,768]{1,0:...) custom-call(bf16[256,768]{1,0:T(8,128)(2,1)} %bitcast.23, ...), custom_call_target="tpu_custom_call" | custom-call | tf_op jit(solution)/shard_map/pallas_call | solution.py:1441
